TPU v7x, 512 devices: a whole 4x8x8 slice. The times are simulated.
512 devices in a mesh: region: 8 (over z), tile: 64 (over y, x, core).
Axes of the slice: x: 4, y: 8, z: 8, core: 2. Of those that a mesh axis runs over, the one named last changes fastest.
Arguments:
- anomalies: bfloat16 [131072, 4096], P(('region', 'tile')), may hold values from -20 to 20
- station_count: int32 [512], P(('region', 'tile')), may hold values from 32 to 256, as said below
- composite_of: int32 [131072], P(('region', 'tile')), may hold values from 0 to 127
Outputs:
- near_corr: float32 [131072, 512], P(('region', 'tile'))
- comp_corr: float32 [131072, 1024], P(('region', 'tile'))
Inputs may be any that keep to these rules, and one draw needn't show every extreme that they name: `station_count`: each tile's live stations fill its first slots; some tile is full in every draw.
All inputs are finite; a program needn't handle non-finite values.
Results may differ from a plain program's by a relative error of at most 0.0048.
Values may be sent and summed in bfloat16 or wider, within the bound.
No kernel may reach another device: no remote copies, remote signals or barrier semaphores. Data moves between devices by JAX's collectives and lax.ppermute only.
A program may use at most 64 MiB of HBM per device.

v0:
```python
import jax
import jax.numpy as jnp
from jax import lax
from jax.sharding import PartitionSpec as P

COMPOSITES = 1024


def with_halo(value, sides, width):
    for axis, dim in sides:
        count, length = (lax.axis_size(axis), value.shape[dim])
        up = [(i, (i + 1) % count) for i in range(count - 1)]
        down = [(j, i) for i, j in up]
        last = lax.slice_in_dim(value, length - width, length, axis=dim)
        leading = lax.slice_in_dim(value, 0, width, axis=dim)
        before = lax.ppermute(last, axis, up)
        after = lax.ppermute(leading, axis, down)
        value = jnp.concatenate([before, value, after], axis=dim)
    return value


def normalize(rows):
    values = rows.astype(jnp.float32)
    center = values - jnp.mean(values, axis=1, keepdims=True)
    return center * lax.rsqrt(jnp.mean(center * center, axis=1, keepdims=True) + 1e-05)


def per_device(anomalies, station_count, composite_of):
    slots, hours = anomalies.shape
    inverse = 1.0 / hours
    live = (jnp.arange(slots) < station_count[0]).astype(jnp.float32)
    zed = (normalize(anomalies) * live[:, None]).astype(jnp.bfloat16)

    def cross(left, right):
        return (
            lax.dot_general(
                left, right, (((1,), (1,)), ((), ())), preferred_element_type=jnp.float32
            )
            * inverse
        )

    comp_reg = COMPOSITES // lax.axis_size("region")
    onehot = (composite_of[None, :] == jnp.arange(comp_reg)[:, None]).astype(jnp.bfloat16)
    sums = lax.psum(jnp.dot(onehot, zed, preferred_element_type=jnp.float32), "tile")
    comps = normalize(sums).astype(jnp.bfloat16)
    comp_corr = cross(zed, lax.all_gather(comps, "region", axis=0, tiled=True))
    padded = with_halo(zed, (("tile", 0),), slots)
    near_corr = jnp.concatenate(
        [cross(zed, padded[:slots]), cross(zed, padded[2 * slots :])], axis=1
    )
    return (near_corr, comp_corr)


def solution(mesh):
    in_specs = (P(("region", "tile"), None), P(("region", "tile")), P(("region", "tile")))
    out_specs = (P(("region", "tile"), None), P(("region", "tile"), None))
    return jax.shard_map(
        per_device, mesh=mesh, in_specs=in_specs, out_specs=out_specs, check_vma=False
    )
```

profile of v0, /device:TPU:1, one launch (start us, length us, event | category | flops | bytes accessed | tf_op | source)
XLA Modules:
  0.0 335.8 jit_solution(7443106080313946282)
XLA Ops:
  7.2 0.0 copy-start
  7.2 0.0 all-reduce.2.cloned.1.call-start
  8.0 2.0 convert_reduce_fusion
  10.0 0.0 copy-done
  10.0 0.7 fusion.2
  10.7 0.0 copy-start.4
  10.7 1.2 fusion.4
  11.9 0.0 copy-start.2
  11.9 1.4 copy-done.2
  13.3 0.0 copy-done.4
  13.3 1.7 fusion.5
  15.0 0.0 all-reduce.2.cloned.1.call-update
  15.1 0.0 all-gather.2.cloned.1.call-start
  15.1 204.7 %all-reduce.2.cloned.1.call-done = f32[128,4096]{1,0:T(8,128)} async-done(((f32[128,4096]{1,0:T(8,128)}), f32[128,4096]{1,0:T(8,128)}) %all-reduce.2.cloned.1.call-update) | async-done | bytes 2097168 | tf_op jit(solution)/shard_map/psum | solution.py:44
  219.8 0.0 copy-start.1
  219.8 1.9 reduce_sum.38
  221.7 0.3 copy-done.1
  222.0 0.4 multiply_reduce_fusion
  222.3 1.3 multiply_convert_fusion
  223.6 0.0 all-gather.2.cloned.1.call-update
  223.7 0.0 copy-start.3
  223.7 4.4 %collective-permute-start.1 = (bf16[256,4096]{1,0:T(8,128)(2,1)}, bf16[256,4096]{1,0:T(8,128)(2,1)S(1)}, u32[]{:S(2)}, u32[]{:S(2)}) collective-permute-start(bf16[256,4096]{1,0:T(8,128)(2,1)} %copy-done.2), channel_id=1, source_target_pairs={{1,0},{2,1},{3,2},{4,3},{5,4},{6,5},{7,6},{8,7},{9,8},{10,9},{11,1... | collective-permute-start | bytes 6291464 | tf_op jit(solution)/shard_map/ppermute | solution.py:17
  228.0 2.6 collective-permute-start
  230.6 22.4 %collective-permute-done.1 = bf16[256,4096]{1,0:T(8,128)(2,1)S(1)} collective-permute-done((bf16[256,4096]{1,0:T(8,128)(2,1)}, bf16[256,4096]{1,0:T(8,128)(2,1)S(1)}, u32[]{:S(2)}, u32[]{:S(2)}) %collective-permute-start.1) | collective-permute-done | bytes 2097184 | tf_op jit(solution)/shard_map/ppermute | solution.py:17
  253.0 2.3 convolution_multiply_fusion.1
  255.4 0.0 collective-permute-done
  255.4 0.0 copy-done.3
  255.4 0.7 convolution_multiply_fusion.2
  256.2 1.0 copy.5
  257.2 65.1 %all-gather.2.cloned.1.call-done = bf16[1024,4096]{1,0:T(8,128)(2,1)} async-done(((bf16[128,4096]{1,0:T(8,128)(2,1)}), bf16[1024,4096]{1,0:T(8,128)(2,1)}) %all-gather.2.cloned.1.call-update) | async-done | bytes 8388624 | tf_op jit(solution)/shard_map/all_gather | solution.py:46
  322.2 6.7 %convolution_multiply_fusion = f32[256,1024]{1,0:T(8,128)} fusion(bf16[256,4096]{1,0:T(8,128)(2,1)S(1)} %copy-done.3, bf16[1024,4096]{1,0:T(8,128)(2,1)} %all-gather.2.cloned.1.call-done), kind=kOutput, calls=%fused_computation.9 | convolution fusion | flops 2147745792 | bytes 11534336 | tf_op jit(solution)/shard_map/dot_general | solution.py:36
  (6 shorter events, 0.1 us)
Async XLA Ops:
  7.2 2.8 copy-start
  7.2 212.6 %all-reduce.2.cloned.1.call-start = ((), (), s32[]{:S(2)}) async-start(), calls=%async_computation | async-start | bytes 4194304 | tf_op jit(solution)/shard_map/psum | solution.py:44
  10.7 2.6 copy-start.4
  11.9 1.4 copy-start.2
  15.1 307.2 %all-gather.2.cloned.1.call-start = ((), (), s32[]{:S(2)}) async-start(), calls=%async_computation.1 | async-start | bytes 9437184 | tf_op jit(solution)/shard_map/all_gather | solution.py:46
  219.8 2.2 copy-start.1
  223.7 31.7 %copy-start.3 = (bf16[256,4096]{1,0:T(8,128)(2,1)S(1)}, bf16[256,4096]{1,0:T(8,128)(2,1)}, u32[]{:S(2)}) copy-start(bf16[256,4096]{1,0:T(8,128)(2,1)} %copy-done.2) | copy-start | bytes 6291460
  223.7 29.4 %collective-permute-start.1 = (bf16[256,4096]{1,0:T(8,128)(2,1)}, bf16[256,4096]{1,0:T(8,128)(2,1)S(1)}, u32[]{:S(2)}, u32[]{:S(2)}) collective-permute-start(bf16[256,4096]{1,0:T(8,128)(2,1)} %copy-done.2), channel_id=1, source_target_pairs={{1,0},{2,1},{3,2},{4,3},{5,4},{6,5},{7,6},{8,7},{9,8},{10,9},{11,1... | collective-permute-start | bytes 6291464 | tf_op jit(solution)/shard_map/ppermute | solution.py:17
  228.0 27.4 %collective-permute-start = (bf16[256,4096]{1,0:T(8,128)(2,1)}, bf16[256,4096]{1,0:T(8,128)(2,1)S(1)}, u32[]{:S(2)}, u32[]{:S(2)}) collective-permute-start(bf16[256,4096]{1,0:T(8,128)(2,1)} %copy-done.2), channel_id=1, source_target_pairs={{0,1},{1,2},{2,3},{3,4},{4,5},{5,6},{6,7},{7,8},{8,9},{9,10},{10,1... | collective-permute-start | bytes 6291464 | tf_op jit(solution)/shard_map/ppermute | solution.py:16
Sparse Core Ops, SparseCore 0:
  15.2 204.5 all-reduce.1
  223.8 98.4 all-gather.1
where the time goes:
time: 336 us
  waiting for transfers between devices  292 us (87%)
  between operations  14.9 us (4%)
  matrix products  11.5 us (3%)
  other arithmetic  7.46 us (2%)
  starting transfers between devices  7.04 us (2%)
    psum x1, waiting for transfers between devices, per_device(): lax.psum(jnp.dot(onehot, zed, preferred_element_type=jnp.float32), 'tile')  205 us
    all_gather x1, waiting for transfers between devices, per_device(): comp_corr = cross(zed, lax.all_gather(comps, 'region', axis=0, tiled=True))  65.1 us
    ppermute x1, waiting for transfers between devices, with_halo(): after = lax.ppermute(leading, axis, down)  22.4 us
    dot_general x3, matrix products, cross(): lax.dot_general(left, right, (((1,), (1,)), ((), ())), preferred_element_...  9.8 us
  transfers between devices with their start and end apart: 4, of which 3 were waited for; matrix products, arithmetic and copies ran while one was open for 1% of the time, Pallas kernels for 0%

commit v1 on v0

v1 whole, which is shorter than its diff:
```python
import functools

import jax
import jax.numpy as jnp
from jax import lax
from jax.experimental import pallas as pl
from jax.experimental.pallas import tpu as pltpu
from jax.sharding import Mesh, PartitionSpec as P

HOURS = 4096
SLOTS = 256
COMP_REG = 128
HALF = COMP_REG // 2
EPS = 1e-05
CHUNK = 512
NCHUNK = HOURS // CHUNK
ROWS = 32
F32 = jnp.float32
BF16 = jnp.bfloat16
SMEM = pl.BlockSpec(memory_space=pltpu.SMEM)
NT = (((1,), (1,)), ((), ()))


def params(mib):
    return pltpu.CompilerParams(vmem_limit_bytes=mib << 20)


VMEM = pl.BlockSpec(memory_space=pltpu.VMEM)
HBM = pl.BlockSpec(memory_space=pltpu.HBM)


def zed_kernel(count, core, ids, x, zed, edge, own, theirs, held, sems):
    steps = SLOTS // ROWS
    rows_of = lambda step: pl.ds(step * ROWS, ROWS)
    copies = [
        pltpu.make_async_copy(x.at[rows_of(step)], held.at[rows_of(step)], sems.at[step]) for step in range(steps)
    ]
    for copy in copies:
        copy.start()
    for step, copy in enumerate(copies):
        copy.wait()
        values = held[rows_of(step), :].astype(F32)
        center = values - jnp.mean(values, axis=1, keepdims=True)
        scale = lax.rsqrt(jnp.mean(center * center, axis=1, keepdims=True) + EPS)
        slot = step * ROWS + lax.broadcasted_iota(jnp.int32, (ROWS, 1), 0)
        live = (slot < count[0]).astype(F32)
        rows = (center * scale * live).astype(BF16)
        zed[rows_of(step), :] = rows
        edge[rows_of(step), :] = jnp.where(core[0] == 0, rows[:, : HOURS // 2], rows[:, HOURS // 2 :])

    index = lax.broadcasted_iota(jnp.int32, (COMP_REG, SLOTS), 0)
    index = (index + HALF * core[0]) & (COMP_REG - 1)
    hot = (ids[...] == index).astype(F32).astype(BF16)
    for k in range(NCHUNK):
        part = jnp.dot(hot, zed[:, k * CHUNK : (k + 1) * CHUNK], preferred_element_type=F32)
        own[k] = part[:HALF]
        theirs[k] = part[HALF:].astype(BF16)


def make_zed(count, core, ids, x):
    block = (NCHUNK, HALF, CHUNK)
    return pl.pallas_call(
        zed_kernel,
        in_specs=[SMEM, SMEM, VMEM, HBM],
        out_specs=[VMEM] * 4,
        out_shape=[
            jax.ShapeDtypeStruct((SLOTS, HOURS), BF16),
            jax.ShapeDtypeStruct((SLOTS, HOURS // 2), BF16),
            jax.ShapeDtypeStruct(block, F32),
            jax.ShapeDtypeStruct(block, BF16),
        ],
        scratch_shapes=[pltpu.VMEM((SLOTS, HOURS), BF16), pltpu.SemaphoreType.DMA((SLOTS // ROWS,))],
        compiler_params=params(24),
        cost_estimate=pl.CostEstimate(flops=300_000_000, bytes_accessed=6 << 20, transcendentals=0),
        name="normalize_and_sum",
    )(count, core, ids, x)


def lane_sums(block):
    wide = block[:, :128]
    for k in range(1, block.shape[1] // 128):
        wide = wide + block[:, k * 128 : (k + 1) * 128]
    return wide


def near_kernel(core, zed, other, halo, same, mine, theirs, zsum, osum, wide):
    z = zed[...]
    same[...] = lax.dot_general(z, other[...], NT, preferred_element_type=F32) * (1.0 / HOURS)

    @pl.when(core[0] == 0)
    def _():
        half = zed[:, HOURS // 2 :]
        mine[...] = lax.dot_general(half, halo[...], NT, preferred_element_type=F32)
        theirs[...] = lax.dot_general(halo[...], half, NT, preferred_element_type=F32)

    @pl.when(core[0] != 0)
    def _():
        half = zed[:, : HOURS // 2]
        mine[...] = lax.dot_general(half, halo[...], NT, preferred_element_type=F32)
        theirs[...] = lax.dot_general(halo[...], half, NT, preferred_element_type=F32)

    for rows, out in ((zed, zsum), (other, osum)):
        wide[...] = lane_sums(rows[:, :CHUNK].astype(F32))
        for k in range(1, NCHUNK):
            wide[...] += lane_sums(rows[:, k * CHUNK : (k + 1) * CHUNK].astype(F32))
        out[...] = jnp.broadcast_to(jnp.sum(wide[...], axis=1, keepdims=True), out.shape)


def make_near(place, zed, other, halo):
    square = jax.ShapeDtypeStruct((SLOTS, SLOTS), F32)
    return pl.pallas_call(
        near_kernel,
        in_specs=[SMEM, VMEM, VMEM, VMEM],
        out_specs=[VMEM] * 5,
        out_shape=[square] * 3 + [jax.ShapeDtypeStruct((SLOTS, 128), F32)] * 2,
        scratch_shapes=[pltpu.VMEM((SLOTS, 128), F32)],
        compiler_params=params(16),
        cost_estimate=pl.CostEstimate(flops=1_073_741_824, bytes_accessed=6 << 20, transcendentals=0),
        name="neighbour_correlation",
    )(place, zed, other, halo)


def near_sum_kernel(core, same, mine, got, near):
    at = pl.multiple_of(core[0] * SLOTS, SLOTS)
    near[:, pl.ds(at, SLOTS)] = (mine[...] + got[...]) * (1.0 / HOURS)
    near[:, pl.ds(SLOTS - at, SLOTS)] = same[...]


def near_sum(place, same, mine, got):
    return pl.pallas_call(
        near_sum_kernel,
        in_specs=[SMEM, VMEM, VMEM, VMEM],
        out_specs=VMEM,
        out_shape=jax.ShapeDtypeStruct((SLOTS, 2 * SLOTS), F32),
        compiler_params=params(8),
        cost_estimate=pl.CostEstimate(flops=1 << 18, bytes_accessed=5 << 18, transcendentals=0),
        name="neighbour_sum",
    )(place, same, mine, got)


COMPS = 8 * HALF


def whole(block):
    return block[...].reshape(COMPS, CHUNK)


def hours_of(at, delta):
    return pl.ds(pl.multiple_of(((at + delta) & 7) * CHUNK, CHUNK), CHUNK)


def times(left, right):
    return lax.dot_general(left, right, NT, preferred_element_type=F32)


def early_kernel(place, *refs):
    blocks, (zed, other, mine, theirs, s_1, s_2) = refs[:7], refs[7:]
    core, at = place[0], place[1]

    def add(hours, rows, start):
        wide = rows.astype(F32)
        for out, new in (
            (mine, times(zed[:, hours], rows)),
            (theirs, times(other[:, hours], rows)),
            (s_1, lane_sums(wide)),
            (s_2, lane_sums(wide * wide)),
        ):
            out[...] = new if start else out[...] + new

    @pl.when(core == 0)
    def _():
        for i, (block, delta) in enumerate(zip(blocks, (0, 7, 1, 6, 2, 5, 3))):
            add(hours_of(at, delta), whole(block), i == 0)

    @pl.when(core != 0)
    def _():
        for k in range(NCHUNK):
            rows = jnp.concatenate([block[k] for block in blocks] + [blocks[0][k]], axis=0)
            add(slice(k * CHUNK, (k + 1) * CHUNK), rows, k == 0)


def late_kernel(here, place, far_a, far_b, zed, zsum, acc, *refs):
    core, at = place[0], place[1]
    last = slice(COMPS - HALF, COMPS)
    if here:
        e_1, e_2, out, stats, s_1, s_2 = refs
        s_1[...], s_2[...] = e_1[...], e_2[...]
    else:
        stats, out = refs

    @pl.when(core == 0)
    def _():
        rows = jnp.concatenate([far_a[...], far_b[...]], axis=0).reshape(COMPS, CHUNK)
        out[...] = acc[...] + times(zed[:, hours_of(at, 4)], rows)
        if here:
            wide = rows.astype(F32)
            s_1[...] += lane_sums(wide)
            s_2[...] += lane_sums(wide * wide)

    @pl.when(core != 0)
    def _():
        total = jnp.zeros((SLOTS, 128), F32)
        wide_1 = wide_2 = jnp.zeros((HALF, 128), F32)
        for k in range(NCHUNK):
            rows = far_a[k] if k < 4 else far_b[k - 4]
            total = total + times(zed[:, k * CHUNK : (k + 1) * CHUNK], jnp.concatenate([rows, rows], axis=0))
            if here:
                wide = rows.astype(F32)
                wide_1, wide_2 = wide_1 + lane_sums(wide), wide_2 + lane_sums(wide * wide)
        if here:
            s_1[last], s_2[last] = wide_1, wide_2
        out[:, : COMPS - 128] = acc[:, : COMPS - 128]
        first = lax.broadcasted_iota(jnp.int32, (SLOTS, 128), 1) < HALF
        out[:, COMPS - 128 :] = jnp.where(first, acc[:, COMPS - 128 :], total)

    if here:
        mean = jnp.sum(s_1[...].T, axis=0, keepdims=True) * (1.0 / HOURS)
        square = jnp.sum(s_2[...].T, axis=0, keepdims=True) * (1.0 / HOURS)
        inv = lax.rsqrt(jnp.maximum(square - mean * mean, 0.0) + EPS) * (1.0 / HOURS)
        stats[0:8, :] = jnp.broadcast_to(mean, (8, COMPS))
        stats[8:16, :] = jnp.broadcast_to(inv, (8, COMPS))
    else:
        mean = stats[0:1, :]
        inv = stats[8:9, :]
    out[...] = (out[...] - zsum[:, 0:1] * mean) * inv


def shape(*dims):
    return jax.ShapeDtypeStruct(dims, F32)


def make_early(place, blocks, zed, other):
    return pl.pallas_call(
        early_kernel,
        in_specs=[SMEM] + [VMEM] * 9,
        out_specs=[VMEM] * 4,
        out_shape=[shape(SLOTS, COMPS)] * 2 + [shape(COMPS, 128)] * 2,
        compiler_params=params(24),
        cost_estimate=pl.CostEstimate(flops=15 << 27, bytes_accessed=9 << 20, transcendentals=0),
        name="early_composites",
    )(place, *blocks, zed, other)


def make_late(place, blocks, zed, zsum, acc, sums=None, stats=None):
    here = stats is None
    scratch = [pltpu.VMEM((COMPS, 128), F32)] * 2 if here else []
    extra = list(sums) if here else [stats]
    return pl.pallas_call(
        functools.partial(late_kernel, here),
        in_specs=[SMEM] + [VMEM] * (5 + len(extra)),
        out_specs=[VMEM] * (2 if here else 1),
        out_shape=[shape(SLOTS, COMPS)] + ([shape(16, COMPS)] if here else []),
        scratch_shapes=scratch,
        compiler_params=params(24),
        cost_estimate=pl.CostEstimate(flops=1 << 27, bytes_accessed=4 << 20, transcendentals=0),
        name="late_composites",
    )(place, *blocks, zed, zsum, acc, *extra)


def merge_kernel(place, mine, got, out):
    core, z, step = place[0], place[2], pl.program_id(0)
    first = lax.broadcasted_iota(jnp.int32, (SLOTS, 128), 1) < HALF
    tile = pl.ds(pl.multiple_of(step * 128, 128), 128)
    low = jnp.where(core == 0, mine[:, tile], got[:, tile])
    for odd in range(2):
        d = (2 * step + odd - z) & 7
        slot = jnp.where(d == 0, 0, jnp.where(d == 4, 7, jnp.where(d < 4, 2 * d, 15 - 2 * d)))
        tile = pl.ds(pl.multiple_of((slot >> 1) * 128, 128), 128)
        rows = jnp.where(core == 0, got[:, tile], mine[:, tile])
        high = jnp.where((slot & 1) == 1, rows, pltpu.roll(rows, HALF, 1))
        out[:, odd * 128 : odd * 128 + 128] = jnp.where(first, pltpu.roll(low, HALF, 1) if odd else low, high)


def merge(place, mine, got):
    return pl.pallas_call(
        merge_kernel,
        grid=(4,),
        in_specs=[SMEM, VMEM, VMEM],
        out_specs=pl.BlockSpec((SLOTS, 256), lambda i: (0, i)),
        out_shape=shape(SLOTS, 1024),
        compiler_params=params(8),
        cost_estimate=pl.CostEstimate(flops=1 << 20, bytes_accessed=2 << 20, transcendentals=0),
        name="merge_halves",
    )(place, mine, got)


def groups_and_rings():
    number = lambda z, y, x, c: ((z * 8 + y) * 4 + x) * 2 + c
    line = [(i, x) for i in range(8) for x in range(4)]
    groups = [[number(z, y, x, 0) for z, x in line] for y in range(8)]
    groups += [[number(z, y, x, 1) for y, x in line] for z in range(8)]
    up = []
    for z in range(8):
        for y in range(8):
            for x in range(4):
                up.append((number(z, y, x, 0), number(z, (y + 1) % 8, x, 0)))
                up.append((number(z, y, x, 1), number((z + 1) % 8, y, x, 1)))
    return groups, up, [(j, i) for i, j in up]


def per_device(anomalies, station_count, composite_of):
    core, y, z = (lax.axis_index(name).astype(jnp.int32) for name in ("c", "y", "z"))
    place = jnp.stack([core, jnp.where(core == 0, y, z), z])
    swap = [(0, 1), (1, 0)]
    every = ("z", "y", "x", "c")
    together = lax.optimization_barrier
    groups, up, down = groups_and_rings()
    zed, edge, own, theirs = make_zed(station_count, place, composite_of.reshape(1, SLOTS), anomalies)

    got = lax.ppermute(theirs, "c", swap)
    part = (own + got.astype(F32)).astype(BF16).reshape(32, 16, CHUNK)
    part, zed, edge = together((part, zed, edge))
    blocks = lax.all_to_all(part, ("y", "x"), split_axis=0, concat_axis=0, tiled=True)
    block = jnp.sum(blocks.astype(F32), axis=0).astype(BF16)

    across = [(i, i + 1) for i in range(1, 63, 2)]
    across += [(j, i) for i, j in across]
    other = lax.ppermute(zed, "c", swap)
    halo = lax.ppermute(edge, every[1:], across)
    same, near_mine, near_theirs, zsum, osum = make_near(place, zed, other, halo)
    near_got = lax.ppermute(near_theirs, every[1:], across)

    spread = jnp.broadcast_to(block, (32, 16, CHUNK))
    first = lax.all_to_all(spread, every, split_axis=0, concat_axis=0, axis_index_groups=groups, tiled=True)
    first, near_got = together((first.reshape(8, HALF, CHUNK), near_got))
    before, after = [first], [first]
    for step in range(3):
        before.append(lax.ppermute(before[step], every, up))
        after.append(lax.ppermute(after[step], every, down))
    far = [lax.ppermute(before[3][:4], every, up), lax.ppermute(after[3][4:], every, down)]

    near_corr = near_sum(place, same, near_mine, near_got)
    near_blocks = [first, before[1], after[1], before[2], after[2], before[3], after[3]]
    early = make_early(place, near_blocks, zed, other)
    far[0], near_corr = together((far[0], near_corr))
    for_other, stats = make_late(place, far, other, osum, early[1], sums=early[2:])
    back = lax.ppermute(for_other, "c", swap)
    (mine,) = make_late(place, far, zed, zsum, early[0], stats=stats)
    return near_corr, merge(place, mine, back)


def solution(mesh):
    grid = Mesh(mesh.devices.reshape(8, 8, 4, 2), ("z", "y", "x", "c"))
    axes = ("z", "y", "x", "c")
    return jax.shard_map(
        per_device,
        mesh=grid,
        in_specs=(P(axes, None), P(axes), P(axes)),
        out_specs=(P(axes, None), P(axes, None)),
        check_vma=False,
    )
```

time: 336 us -> 130 us (0.39)
  waiting for transfers between devices: 292 us -> 34.3 us
  starting transfers between devices: 7.04 us -> 68.2 us
  Pallas kernels: 0 us -> 20.8 us
  between operations: 14.9 us -> 1.53 us
  matrix products: 11.5 us -> 0 us
  other arithmetic: 7.46 us -> 1.13 us
    psum x1 -> x0, waiting for transfers between devices: 205 us -> none  [per_device(): lax.psum(jnp.dot(onehot, zed, preferred_element_type=jnp.float32), 'tile')]
    all_gather x1 -> x0, waiting for transfers between devices: 65.1 us -> none  [per_device(): comp_corr = cross(zed, lax.all_gather(comps, 'region', axis=0, tiled=True))]
    ppermute x2 -> x13, starting transfers between devices: 6.96 us -> 59 us  [the longest x1 12.9 us: per_device(): near_got = lax.ppermute(near_theirs, every[1:], across)]
    pallas_call x0 -> x7, Pallas kernels: none -> 20.8 us  [the longest x1 4.39 us: make_zed(): pl.pallas_call(zed_kernel, in_specs=[SMEM, SMEM, VMEM, HBM], out_specs=[V...]
    all_to_all x0 -> x2, waiting for transfers between devices: none -> 13 us  [the longest x1 13 us: per_device(): lax.all_to_all(part, ('y', 'x'), split_axis=0, concat_axis=0, tiled=True)]
    dot_general x4 -> x0, matrix products: 11.5 us -> none  [the longest x3 9.8 us: cross(): lax.dot_general(left, right, (((1,), (1,)), ((), ())), preferred_element_...]
    all_to_all x0 -> x2, starting transfers between devices: none -> 9.2 us  [the longest x1 4.89 us: per_device(): lax.all_to_all(spread, every, split_axis=0, concat_axis=0, axis_index_gro...]
    reduce_sum x4 -> x1, other arithmetic: 4.93 us -> 0.09 us  [per_device(): block = jnp.sum(blocks.astype(F32), axis=0).astype(BF16)]
  transfers between devices with their start and end apart: 4 -> 15, of which waited for: 3 -> 7; matrix products, arithmetic and copies ran while one was open for 1% -> 1% of each run, Pallas kernels for 0% -> 9%
where the time goes in v1:
time: 130 us
  starting transfers between devices  68.2 us (52%)
  waiting for transfers between devices  34.3 us (26%)
  Pallas kernels  20.8 us (16%)
  local copies, waits for them, and re-layouts  3.82 us (3%)
  between operations  1.53 us (1%)
    ppermute x3, waiting for transfers between devices, per_device(): before.append(lax.ppermute(before[step], every, up))  14.7 us
    all_to_all x1, waiting for transfers between devices, per_device(): lax.all_to_all(part, ('y', 'x'), split_axis=0, concat_axis=0, tiled=True)  13 us
    ppermute x1, starting transfers between devices, per_device(): near_got = lax.ppermute(near_theirs, every[1:], across)  12.9 us
    ppermute x3, starting transfers between devices, per_device(): after.append(lax.ppermute(after[step], every, down))  12.6 us
    ppermute x1, starting transfers between devices, per_device(): got = lax.ppermute(theirs, 'c', swap)  8.79 us
    ppermute x3, starting transfers between devices, per_device(): before.append(lax.ppermute(before[step], every, up))  6.89 us
    ppermute x1, starting transfers between devices, per_device(): back = lax.ppermute(for_other, 'c', swap)  5.33 us
    all_to_all x1, starting transfers between devices, per_device(): lax.all_to_all(spread, every, split_axis=0, concat_axis=0, axis_index_gro...  4.89 us
  transfers between devices with their start and end apart: 15, of which 7 were waited for; matrix products, arithmetic and copies ran while one was open for 1% of the time, Pallas kernels for 9%

profile of v1, /device:TPU:1, one launch (start us, length us, event | category | flops | bytes accessed | tf_op | source)
XLA Modules:
  0.0 129.7 jit_solution(1020771111384081626)
XLA Ops:
  1.3 0.1 pad_add_fusion.core.place
  1.4 0.0 copy-start
  1.4 1.6 %copy-done = bf16[256,4096]{1,0:T(8,128)(2,1)S(1)} copy-done((bf16[256,4096]{1,0:T(8,128)(2,1)S(1)}, bf16[256,4096]{1,0:T(8,128)(2,1)}, u32[]{:S(2)}) %copy-start) | copy-done | bytes 2097176
  3.0 0.0 copy-start.3
  3.0 0.7 copy-done.3
  3.6 4.4 %normalize_and_sum.1 = (bf16[256,4096]{1,0:T(8,128)(2,1)S(1)}, bf16[256,2048]{1,0:T(8,128)(2,1)}, f32[8,64,512]{2,1,0:T(8,128)S(1)}, bf16[8,64,512]{2,1,0:T(8,128)(2,1)S(1)}) custom-call(s32[1]{0:T(128)S(6)} %copy.5.count, s32[3]{0:T(128)S(1)} %pad_add_fusion.core.place, s32[1,256]{1,0:T(1,128)S(1)} %bitcast.9, bf16[256,4096]{1,0:T(8,128)(2,1)S(1)} %copy-done), custom_call_target="tpu_custom_call" | custom-call | flops 300000000 | bytes 6291456 | tf_op jit(solution)/shard_map/normalize_and_sum/pallas_call | solution.py:62
  8.0 8.8 %collective-permute-start = (bf16[8,64,512]{2,1,0:T(8,128)(2,1)S(1)}, bf16[8,64,512]{2,1,0:T(8,128)(2,1)S(1)}, u32[]{:S(2)}, u32[]{:S(2)}) collective-permute-start(bf16[8,64,512]{2,1,0:T(8,128)(2,1)S(1)} %get-tuple-element.25), channel_id=1, source_target_pairs={{0,1},{1,0},{2,3},{3,2},{4,5},{5,4},{6,7},{7,6},{8,9},{9,8},{10,11... | collective-permute-start | bytes 1572872 | tf_op jit(solution)/shard_map/ppermute | solution.py:310
  16.8 1.5 %collective-permute-done = bf16[8,64,512]{2,1,0:T(8,128)(2,1)S(1)} collective-permute-done((bf16[8,64,512]{2,1,0:T(8,128)(2,1)S(1)}, bf16[8,64,512]{2,1,0:T(8,128)(2,1)S(1)}, u32[]{:S(2)}, u32[]{:S(2)}) %collective-permute-start) | collective-permute-done | bytes 524320 | tf_op jit(solution)/shard_map/ppermute | solution.py:310
  18.3 1.0 add_convert_fusion
  19.3 2.3 %collective-permute-start.1 = (bf16[256,4096]{1,0:T(8,128)(2,1)S(1)}, bf16[256,4096]{1,0:T(8,128)(2,1)}, u32[]{:S(2)}, u32[]{:S(2)}) collective-permute-start(bf16[256,4096]{1,0:T(8,128)(2,1)S(1)} %get-tuple-element.29.zed.refs_7_), channel_id=1, source_target_pairs={{0,1},{1,0},{2,3},{3,2},{4,5},{5,4},{6,7},{7,6},{8,9},{9,8},{10,11... | collective-permute-start | bytes 6291464 | tf_op jit(solution)/shard_map/ppermute | solution.py:318
  21.6 4.3 %all-to-all-start = ((bf16[32,16,512]{2,1,0:T(8,128)(2,1)}), bf16[32,16,512]{2,1,0:T(8,128)(2,1)S(1)}, u32[]{:S(2)}, u32[]{:S(2)}) async-start(bf16[32,16,512]{2,1,0:T(8,128)(2,1)} %bitcast.4), calls=%async_computation | async-start | bytes 1048576 | tf_op jit(solution)/shard_map/all_to_all | solution.py:313
  25.9 3.7 %collective-permute-start.2 = (bf16[256,2048]{1,0:T(8,128)(2,1)}, bf16[256,2048]{1,0:T(8,128)(2,1)}, u32[]{:S(2)}, u32[]{:S(2)}) collective-permute-start(bf16[256,2048]{1,0:T(8,128)(2,1)} %get-tuple-element.30), channel_id=1, source_target_pairs={{1,2},{3,4},{5,6},{7,8},{9,10},{11,12},{13,14},{15,16},{17,18},{19... | collective-permute-start | bytes 3145736 | tf_op jit(solution)/shard_map/ppermute | solution.py:319
  29.6 13.0 %all-to-all-done = bf16[32,16,512]{2,1,0:T(8,128)(2,1)S(1)} async-done(((bf16[32,16,512]{2,1,0:T(8,128)(2,1)}), bf16[32,16,512]{2,1,0:T(8,128)(2,1)S(1)}, u32[]{:S(2)}, u32[]{:S(2)}) %all-to-all-start) | async-done | bytes 524320 | tf_op jit(solution)/shard_map/all_to_all | solution.py:313
  42.6 0.1 reduce_sum.12
  42.7 0.9 broadcast_in_dim.3
  43.6 4.9 %all-to-all-start.1 = ((bf16[32,16,512]{2,1,0:T(8,128)(2,1)}), bf16[32,16,512]{2,1,0:T(8,128)(2,1)S(1)}, u32[]{:S(2)}, u32[]{:S(2)}) async-start(bf16[32,16,512]{2,1,0:T(8,128)(2,1)} %broadcast_in_dim.3), calls=%async_computation.1 | async-start | bytes 1048576 | tf_op jit(solution)/shard_map/all_to_all | solution.py:324
  48.5 0.0 collective-permute-done.2.halo
  48.5 0.0 collective-permute-done.1.other.refs_8_.zed
  48.5 4.1 %neighbour_correlation.1 = (f32[256,256]{1,0:T(8,128)S(1)}, f32[256,256]{1,0:T(8,128)S(1)}, f32[256,256]{1,0:T(8,128)}, f32[256,128]{1,0:T(8,128)S(1)}, f32[256,128]{1,0:T(8,128)S(1)}) custom-call(s32[3]{0:T(128)S(1)} %pad_add_fusion.core.place, bf16[256,4096]{1,0:T(8,128)(2,1)S(1)} %get-tuple-element.29.zed.refs_7_, ...), custom_call_target="tpu_custom_call" | custom-call | flops 1073741824 | bytes 6291456 | tf_op jit(solution)/shard_map/neighbour_correlation/pallas_call | solution.py:111
  52.6 0.0 copy-start.1
  52.6 0.7 copy-done.1
  53.2 12.9 %collective-permute-start.3 = (f32[256,256]{1,0:T(8,128)}, f32[256,256]{1,0:T(8,128)S(1)}, u32[]{:S(2)}, u32[]{:S(2)}) collective-permute-start(f32[256,256]{1,0:T(8,128)} %get-tuple-element.31), channel_id=1, source_target_pairs={{1,2},{3,4},{5,6},{7,8},{9,10},{11,12},{13,14},{15,16},{17,18},{19... | collective-permute-start | bytes 786440 | tf_op jit(solution)/shard_map/ppermute | solution.py:321
  66.2 0.0 all-to-all-done.1
  66.2 4.9 %collective-permute-done.3.got = f32[256,256]{1,0:T(8,128)S(1)} collective-permute-done((f32[256,256]{1,0:T(8,128)}, f32[256,256]{1,0:T(8,128)S(1)}, u32[]{:S(2)}, u32[]{:S(2)}) %collective-permute-start.3) | collective-permute-done | bytes 262176 | tf_op jit(solution)/shard_map/ppermute | solution.py:321
  71.1 3.1 %collective-permute-start.4 = (bf16[8,64,512]{2,1,0:T(8,128)(2,1)S(1)}, bf16[8,64,512]{2,1,0:T(8,128)(2,1)S(1)}, u32[]{:S(2)}, u32[]{:S(2)}) collective-permute-start(bf16[8,64,512]{2,1,0:T(8,128)(2,1)S(1)} %bitcast.6), channel_id=1, source_target_pairs={{0,8},{1,65},{2,10},{3,67},{4,12},{5,69},{6,14},{7,71},{8,16},{9,7... | collective-permute-start | bytes 1572872 | tf_op jit(solution)/shard_map/ppermute | solution.py:328
  74.1 3.4 %collective-permute-start.8 = (bf16[8,64,512]{2,1,0:T(8,128)(2,1)S(1)}, bf16[8,64,512]{2,1,0:T(8,128)(2,1)S(1)}, u32[]{:S(2)}, u32[]{:S(2)}) collective-permute-start(bf16[8,64,512]{2,1,0:T(8,128)(2,1)S(1)} %bitcast.7), channel_id=1, source_target_pairs={{8,0},{65,1},{10,2},{67,3},{12,4},{69,5},{14,6},{71,7},{16,8},{73,... | collective-permute-start | bytes 1572872 | tf_op jit(solution)/shard_map/ppermute | solution.py:329
  77.6 4.9 %collective-permute-done.4.refs_1_ = bf16[8,64,512]{2,1,0:T(8,128)(2,1)S(1)} collective-permute-done((bf16[8,64,512]{2,1,0:T(8,128)(2,1)S(1)}, bf16[8,64,512]{2,1,0:T(8,128)(2,1)S(1)}, u32[]{:S(2)}, u32[]{:S(2)}) %collective-permute-start.4) | collective-permute-done | bytes 524320 | tf_op jit(solution)/shard_map/ppermute | solution.py:328
  82.5 1.9 %collective-permute-start.5 = (bf16[8,64,512]{2,1,0:T(8,128)(2,1)S(1)}, bf16[8,64,512]{2,1,0:T(8,128)(2,1)S(1)}, u32[]{:S(2)}, u32[]{:S(2)}) collective-permute-start(bf16[8,64,512]{2,1,0:T(8,128)(2,1)S(1)} %collective-permute-done.4.refs_1_), channel_id=1, source_target_pairs={{0,8},{1,65},{2,10},{3,67},{4,12},{5,69},{6,14},{7,71},{8,16},{9,7... | collective-permute-start | bytes 1572872 | tf_op jit(solution)/shard_map/ppermute | solution.py:328
  84.4 0.0 collective-permute-done.8.refs_2_
  84.4 4.6 %collective-permute-start.9 = (bf16[8,64,512]{2,1,0:T(8,128)(2,1)S(1)}, bf16[8,64,512]{2,1,0:T(8,128)(2,1)S(1)}, u32[]{:S(2)}, u32[]{:S(2)}) collective-permute-start(bf16[8,64,512]{2,1,0:T(8,128)(2,1)S(1)} %collective-permute-done.8.refs_2_), channel_id=1, source_target_pairs={{8,0},{65,1},{10,2},{67,3},{12,4},{69,5},{14,6},{71,7},{16,8},{73,... | collective-permute-start | bytes 1572872 | tf_op jit(solution)/shard_map/ppermute | solution.py:329
  89.0 4.9 %collective-permute-done.5.refs_3_ = bf16[8,64,512]{2,1,0:T(8,128)(2,1)S(1)} collective-permute-done((bf16[8,64,512]{2,1,0:T(8,128)(2,1)S(1)}, bf16[8,64,512]{2,1,0:T(8,128)(2,1)S(1)}, u32[]{:S(2)}, u32[]{:S(2)}) %collective-permute-start.5) | collective-permute-done | bytes 524320 | tf_op jit(solution)/shard_map/ppermute | solution.py:328
  93.9 1.9 %collective-permute-start.6 = (bf16[8,64,512]{2,1,0:T(8,128)(2,1)S(1)}, bf16[8,64,512]{2,1,0:T(8,128)(2,1)S(1)}, u32[]{:S(2)}, u32[]{:S(2)}) collective-permute-start(bf16[8,64,512]{2,1,0:T(8,128)(2,1)S(1)} %collective-permute-done.5.refs_3_), channel_id=1, source_target_pairs={{0,8},{1,65},{2,10},{3,67},{4,12},{5,69},{6,14},{7,71},{8,16},{9,7... | collective-permute-start | bytes 1572872 | tf_op jit(solution)/shard_map/ppermute | solution.py:328
  95.8 0.0 collective-permute-done.9.refs_4_
  95.8 4.6 %collective-permute-start.10 = (bf16[8,64,512]{2,1,0:T(8,128)(2,1)S(1)}, bf16[8,64,512]{2,1,0:T(8,128)(2,1)S(1)}, u32[]{:S(2)}, u32[]{:S(2)}) collective-permute-start(bf16[8,64,512]{2,1,0:T(8,128)(2,1)S(1)} %collective-permute-done.9.refs_4_), channel_id=1, source_target_pairs={{8,0},{65,1},{10,2},{67,3},{12,4},{69,5},{14,6},{71,7},{16,8},{73,... | collective-permute-start | bytes 1572872 | tf_op jit(solution)/shard_map/ppermute | solution.py:329
  100.4 4.9 %collective-permute-done.6.refs_5_ = bf16[8,64,512]{2,1,0:T(8,128)(2,1)S(1)} collective-permute-done((bf16[8,64,512]{2,1,0:T(8,128)(2,1)S(1)}, bf16[8,64,512]{2,1,0:T(8,128)(2,1)S(1)}, u32[]{:S(2)}, u32[]{:S(2)}) %collective-permute-start.6) | collective-permute-done | bytes 524320 | tf_op jit(solution)/shard_map/ppermute | solution.py:328
  105.3 1.9 %collective-permute-start.7 = (bf16[4,64,512]{2,1,0:T(8,128)(2,1)S(1)}, bf16[4,64,512]{2,1,0:T(8,128)(2,1)S(1)}, u32[]{:S(2)}, u32[]{:S(2)}) collective-permute-start(bf16[4,64,512]{2,1,0:T(8,128)(2,1)S(1)} %slice.8), channel_id=1, source_target_pairs={{0,8},{1,65},{2,10},{3,67},{4,12},{5,69},{6,14},{7,71},{8,16},{9,7... | collective-permute-start | bytes 786440 | tf_op jit(solution)/shard_map/ppermute | solution.py:330
  107.3 0.0 collective-permute-done.10.refs_6_
  107.3 4.6 %collective-permute-start.11 = (bf16[4,64,512]{2,1,0:T(8,128)(2,1)S(1)}, bf16[4,64,512]{2,1,0:T(8,128)(2,1)S(1)}, u32[]{:S(2)}, u32[]{:S(2)}) collective-permute-start(bf16[4,64,512]{2,1,0:T(8,128)(2,1)S(1)} %slice.9), channel_id=1, source_target_pairs={{8,0},{65,1},{10,2},{67,3},{12,4},{69,5},{14,6},{71,7},{16,8},{73,... | collective-permute-start | bytes 786440 | tf_op jit(solution)/shard_map/ppermute | solution.py:330
  111.9 1.4 %neighbour_sum.1 = f32[256,512]{1,0:T(8,128)} custom-call(s32[3]{0:T(128)S(1)} %pad_add_fusion.core.place, f32[256,256]{1,0:T(8,128)S(1)} %get-tuple-element.33.same, f32[256,256]{1,0:T(8,128)S(1)} %get-tuple-element.34.mine, f32[256,256]{1,0:T(8,128)S(1)} %collective-permute-done.3.got), custom_call_target="tpu_custom_call" | custom-call | flops 262144 | bytes 1310720 | tf_op jit(solution)/shard_map/neighbour_sum/pallas_call | solution.py:130
  113.3 4.3 %early_composites.1 = (f32[256,512]{1,0:T(8,128)S(1)}, f32[256,512]{1,0:T(8,128)S(1)}, f32[512,128]{1,0:T(8,128)S(1)}, f32[512,128]{1,0:T(8,128)S(1)}) custom-call(s32[3]{0:T(128)S(1)} %pad_add_fusion.core.place, bf16[8,64,512]{2,1,0:T(8,128)(2,1)S(1)} %bitcast.8, bf16[8,64,512]{2,1,0:T(8,128)(2,1)S(1)} %collective-permute-done.4.refs_1_, ...), custom_call_target="tpu_custom_call" | custom-call | flops 2013265920 | bytes 9437184 | tf_op jit(solution)/shard_map/early_composites/pallas_call | solution.py:233
  117.6 0.0 collective-permute-done.7.far_a
  117.6 0.0 collective-permute-done.11.far_b
  117.6 0.0 copy-done.2
  117.6 2.6 %late_composites.2 = (f32[256,512]{1,0:T(8,128)S(1)}, f32[16,512]{1,0:T(8,128)S(1)}) custom-call(s32[3]{0:T(128)S(1)} %pad_add_fusion.core.place, bf16[4,64,512]{2,1,0:T(8,128)(2,1)S(1)} %collective-permute-done.7.far_a, bf16[4,64,512]{2,1,0:T(8,128)(2,1)S(1)} %collective-permute-done.11.far_b, bf16[256,4096]{1,0:T(8,128)(2,1)} %collective-permute-done.1.other.refs_8_.zed, ...), custom_call_target="tpu_custom_call" | custom-call | flops 134217728 | bytes 4194304 | tf_op jit(solution)/shard_map/late_composites/pallas_call | solution.py:248
  120.2 5.3 %collective-permute-start.12 = (f32[256,512]{1,0:T(8,128)S(1)}, f32[256,512]{1,0:T(8,128)S(1)}, u32[]{:S(2)}, u32[]{:S(2)}) collective-permute-start(f32[256,512]{1,0:T(8,128)S(1)} %get-tuple-element.45), channel_id=1, source_target_pairs={{0,1},{1,0},{2,3},{3,2},{4,5},{5,4},{6,7},{7,6},{8,9},{9,8},{10,11... | collective-permute-start | bytes 1572872 | tf_op jit(solution)/shard_map/ppermute | solution.py:337
  125.6 1.4 %late_composites.3.mine = f32[256,512]{1,0:T(8,128)S(1)} custom-call(s32[3]{0:T(128)S(1)} %pad_add_fusion.core.place, bf16[4,64,512]{2,1,0:T(8,128)(2,1)S(1)} %collective-permute-done.7.far_a, bf16[4,64,512]{2,1,0:T(8,128)(2,1)S(1)} %collective-permute-done.11.far_b, bf16[256,4096]{1,0:T(8,128)(2,1)S(1)} %get-tuple-element.29.zed.refs_7_, ...), custom_call_target="tpu_custom_call" | custom-call | flops 134217728 | bytes 4194304 | tf_op jit(solution)/shard_map/late_composites/pallas_call | solution.py:248
  127.0 0.1 collective-permute-done.12.got
  127.1 2.6 %merge_halves.1 = f32[256,1024]{1,0:T(8,128)} custom-call(s32[3]{0:T(128)S(1)} %pad_add_fusion.core.place, f32[256,512]{1,0:T(8,128)S(1)} %late_composites.3.mine, f32[256,512]{1,0:T(8,128)S(1)} %collective-permute-done.12.got), custom_call_target="tpu_custom_call" | custom-call | flops 1048576 | bytes 2097152 | tf_op jit(solution)/shard_map/merge_halves/pallas_call | solution.py:275
  (3 shorter events, 0.0 us)
Async XLA Ops:
  1.4 1.6 %copy-start = (bf16[256,4096]{1,0:T(8,128)(2,1)S(1)}, bf16[256,4096]{1,0:T(8,128)(2,1)}, u32[]{:S(2)}) copy-start(bf16[256,4096]{1,0:T(8,128)(2,1)} %x.1) | copy-start | bytes 6291460
  3.0 0.7 copy-start.3
  8.0 10.3 %collective-permute-start = (bf16[8,64,512]{2,1,0:T(8,128)(2,1)S(1)}, bf16[8,64,512]{2,1,0:T(8,128)(2,1)S(1)}, u32[]{:S(2)}, u32[]{:S(2)}) collective-permute-start(bf16[8,64,512]{2,1,0:T(8,128)(2,1)S(1)} %get-tuple-element.25), channel_id=1, source_target_pairs={{0,1},{1,0},{2,3},{3,2},{4,5},{5,4},{6,7},{7,6},{8,9},{9,8},{10,11... | collective-permute-start | bytes 1572872 | tf_op jit(solution)/shard_map/ppermute | solution.py:310
  19.3 29.2 %collective-permute-start.1 = (bf16[256,4096]{1,0:T(8,128)(2,1)S(1)}, bf16[256,4096]{1,0:T(8,128)(2,1)}, u32[]{:S(2)}, u32[]{:S(2)}) collective-permute-start(bf16[256,4096]{1,0:T(8,128)(2,1)S(1)} %get-tuple-element.29.zed.refs_7_), channel_id=1, source_target_pairs={{0,1},{1,0},{2,3},{3,2},{4,5},{5,4},{6,7},{7,6},{8,9},{9,8},{10,11... | collective-permute-start | bytes 6291464 | tf_op jit(solution)/shard_map/ppermute | solution.py:318
  21.6 21.1 %all-to-all-start = ((bf16[32,16,512]{2,1,0:T(8,128)(2,1)}), bf16[32,16,512]{2,1,0:T(8,128)(2,1)S(1)}, u32[]{:S(2)}, u32[]{:S(2)}) async-start(bf16[32,16,512]{2,1,0:T(8,128)(2,1)} %bitcast.4), calls=%async_computation | async-start | bytes 1048576 | tf_op jit(solution)/shard_map/all_to_all | solution.py:313
  25.9 22.6 %collective-permute-start.2 = (bf16[256,2048]{1,0:T(8,128)(2,1)}, bf16[256,2048]{1,0:T(8,128)(2,1)}, u32[]{:S(2)}, u32[]{:S(2)}) collective-permute-start(bf16[256,2048]{1,0:T(8,128)(2,1)} %get-tuple-element.30), channel_id=1, source_target_pairs={{1,2},{3,4},{5,6},{7,8},{9,10},{11,12},{13,14},{15,16},{17,18},{19... | collective-permute-start | bytes 3145736 | tf_op jit(solution)/shard_map/ppermute | solution.py:319
  43.6 22.6 %all-to-all-start.1 = ((bf16[32,16,512]{2,1,0:T(8,128)(2,1)}), bf16[32,16,512]{2,1,0:T(8,128)(2,1)S(1)}, u32[]{:S(2)}, u32[]{:S(2)}) async-start(bf16[32,16,512]{2,1,0:T(8,128)(2,1)} %broadcast_in_dim.3), calls=%async_computation.1 | async-start | bytes 1048576 | tf_op jit(solution)/shard_map/all_to_all | solution.py:324
  52.6 0.7 copy-start.1
  53.2 17.9 %collective-permute-start.3 = (f32[256,256]{1,0:T(8,128)}, f32[256,256]{1,0:T(8,128)S(1)}, u32[]{:S(2)}, u32[]{:S(2)}) collective-permute-start(f32[256,256]{1,0:T(8,128)} %get-tuple-element.31), channel_id=1, source_target_pairs={{1,2},{3,4},{5,6},{7,8},{9,10},{11,12},{13,14},{15,16},{17,18},{19... | collective-permute-start | bytes 786440 | tf_op jit(solution)/shard_map/ppermute | solution.py:321
  71.1 11.4 %collective-permute-start.4 = (bf16[8,64,512]{2,1,0:T(8,128)(2,1)S(1)}, bf16[8,64,512]{2,1,0:T(8,128)(2,1)S(1)}, u32[]{:S(2)}, u32[]{:S(2)}) collective-permute-start(bf16[8,64,512]{2,1,0:T(8,128)(2,1)S(1)} %bitcast.6), channel_id=1, source_target_pairs={{0,8},{1,65},{2,10},{3,67},{4,12},{5,69},{6,14},{7,71},{8,16},{9,7... | collective-permute-start | bytes 1572872 | tf_op jit(solution)/shard_map/ppermute | solution.py:328
  74.1 10.3 %collective-permute-start.8 = (bf16[8,64,512]{2,1,0:T(8,128)(2,1)S(1)}, bf16[8,64,512]{2,1,0:T(8,128)(2,1)S(1)}, u32[]{:S(2)}, u32[]{:S(2)}) collective-permute-start(bf16[8,64,512]{2,1,0:T(8,128)(2,1)S(1)} %bitcast.7), channel_id=1, source_target_pairs={{8,0},{65,1},{10,2},{67,3},{12,4},{69,5},{14,6},{71,7},{16,8},{73,... | collective-permute-start | bytes 1572872 | tf_op jit(solution)/shard_map/ppermute | solution.py:329
  82.5 11.4 %collective-permute-start.5 = (bf16[8,64,512]{2,1,0:T(8,128)(2,1)S(1)}, bf16[8,64,512]{2,1,0:T(8,128)(2,1)S(1)}, u32[]{:S(2)}, u32[]{:S(2)}) collective-permute-start(bf16[8,64,512]{2,1,0:T(8,128)(2,1)S(1)} %collective-permute-done.4.refs_1_), channel_id=1, source_target_pairs={{0,8},{1,65},{2,10},{3,67},{4,12},{5,69},{6,14},{7,71},{8,16},{9,7... | collective-permute-start | bytes 1572872 | tf_op jit(solution)/shard_map/ppermute | solution.py:328
  84.4 11.4 %collective-permute-start.9 = (bf16[8,64,512]{2,1,0:T(8,128)(2,1)S(1)}, bf16[8,64,512]{2,1,0:T(8,128)(2,1)S(1)}, u32[]{:S(2)}, u32[]{:S(2)}) collective-permute-start(bf16[8,64,512]{2,1,0:T(8,128)(2,1)S(1)} %collective-permute-done.8.refs_2_), channel_id=1, source_target_pairs={{8,0},{65,1},{10,2},{67,3},{12,4},{69,5},{14,6},{71,7},{16,8},{73,... | collective-permute-start | bytes 1572872 | tf_op jit(solution)/shard_map/ppermute | solution.py:329
  93.9 11.4 %collective-permute-start.6 = (bf16[8,64,512]{2,1,0:T(8,128)(2,1)S(1)}, bf16[8,64,512]{2,1,0:T(8,128)(2,1)S(1)}, u32[]{:S(2)}, u32[]{:S(2)}) collective-permute-start(bf16[8,64,512]{2,1,0:T(8,128)(2,1)S(1)} %collective-permute-done.5.refs_3_), channel_id=1, source_target_pairs={{0,8},{1,65},{2,10},{3,67},{4,12},{5,69},{6,14},{7,71},{8,16},{9,7... | collective-permute-start | bytes 1572872 | tf_op jit(solution)/shard_map/ppermute | solution.py:328
  95.8 11.4 %collective-permute-start.10 = (bf16[8,64,512]{2,1,0:T(8,128)(2,1)S(1)}, bf16[8,64,512]{2,1,0:T(8,128)(2,1)S(1)}, u32[]{:S(2)}, u32[]{:S(2)}) collective-permute-start(bf16[8,64,512]{2,1,0:T(8,128)(2,1)S(1)} %collective-permute-done.9.refs_4_), channel_id=1, source_target_pairs={{8,0},{65,1},{10,2},{67,3},{12,4},{69,5},{14,6},{71,7},{16,8},{73,... | collective-permute-start | bytes 1572872 | tf_op jit(solution)/shard_map/ppermute | solution.py:329
  105.3 12.2 %collective-permute-start.7 = (bf16[4,64,512]{2,1,0:T(8,128)(2,1)S(1)}, bf16[4,64,512]{2,1,0:T(8,128)(2,1)S(1)}, u32[]{:S(2)}, u32[]{:S(2)}) collective-permute-start(bf16[4,64,512]{2,1,0:T(8,128)(2,1)S(1)} %slice.8), channel_id=1, source_target_pairs={{0,8},{1,65},{2,10},{3,67},{4,12},{5,69},{6,14},{7,71},{8,16},{9,7... | collective-permute-start | bytes 786440 | tf_op jit(solution)/shard_map/ppermute | solution.py:330
  107.3 10.3 %collective-permute-start.11 = (bf16[4,64,512]{2,1,0:T(8,128)(2,1)S(1)}, bf16[4,64,512]{2,1,0:T(8,128)(2,1)S(1)}, u32[]{:S(2)}, u32[]{:S(2)}) collective-permute-start(bf16[4,64,512]{2,1,0:T(8,128)(2,1)S(1)} %slice.9), channel_id=1, source_target_pairs={{8,0},{65,1},{10,2},{67,3},{12,4},{69,5},{14,6},{71,7},{16,8},{73,... | collective-permute-start | bytes 786440 | tf_op jit(solution)/shard_map/ppermute | solution.py:330
  113.3 4.3 %copy-start.2 = (f32[256,128]{1,0:T(8,128)S(1)}, f32[256,128]{1,0:T(8,128)}, u32[]{:S(2)}) copy-start(f32[256,128]{1,0:T(8,128)} %copy-done.1) | copy-start | bytes 393220
  120.2 6.9 %collective-permute-start.12 = (f32[256,512]{1,0:T(8,128)S(1)}, f32[256,512]{1,0:T(8,128)S(1)}, u32[]{:S(2)}, u32[]{:S(2)}) collective-permute-start(f32[256,512]{1,0:T(8,128)S(1)} %get-tuple-element.45), channel_id=1, source_target_pairs={{0,1},{1,0},{2,3},{3,2},{4,5},{5,4},{6,7},{7,6},{8,9},{9,8},{10,11... | collective-permute-start | bytes 1572872 | tf_op jit(solution)/shard_map/ppermute | solution.py:337

commit v2 on v1

--- a/solution.py
+++ b/solution.py
@@ -15,6 +15,7 @@
 CHUNK = 512
 NCHUNK = HOURS // CHUNK
 ROWS = 32
+MERGE = 64
 F32 = jnp.float32
 BF16 = jnp.bfloat16
 SMEM = pl.BlockSpec(memory_space=pltpu.SMEM)
@@ -70,7 +71,7 @@
             jax.ShapeDtypeStruct(block, BF16),
         ],
         scratch_shapes=[pltpu.VMEM((SLOTS, HOURS), BF16), pltpu.SemaphoreType.DMA((SLOTS // ROWS,))],
-        compiler_params=params(24),
+        compiler_params=params(48),
         cost_estimate=pl.CostEstimate(flops=300_000_000, bytes_accessed=6 << 20, transcendentals=0),
         name="normalize_and_sum",
     )(count, core, ids, x)
@@ -83,59 +84,57 @@
     return wide
 
 
-def near_kernel(core, zed, other, halo, same, mine, theirs, zsum, osum, wide):
-    z = zed[...]
-    same[...] = lax.dot_general(z, other[...], NT, preferred_element_type=F32) * (1.0 / HOURS)
-
-    @pl.when(core[0] == 0)
-    def _():
-        half = zed[:, HOURS // 2 :]
-        mine[...] = lax.dot_general(half, halo[...], NT, preferred_element_type=F32)
-        theirs[...] = lax.dot_general(halo[...], half, NT, preferred_element_type=F32)
-
-    @pl.when(core[0] != 0)
-    def _():
-        half = zed[:, : HOURS // 2]
-        mine[...] = lax.dot_general(half, halo[...], NT, preferred_element_type=F32)
-        theirs[...] = lax.dot_general(halo[...], half, NT, preferred_element_type=F32)
-
-    for rows, out in ((zed, zsum), (other, osum)):
-        wide[...] = lane_sums(rows[:, :CHUNK].astype(F32))
-        for k in range(1, NCHUNK):
-            wide[...] += lane_sums(rows[:, k * CHUNK : (k + 1) * CHUNK].astype(F32))
-        out[...] = jnp.broadcast_to(jnp.sum(wide[...], axis=1, keepdims=True), out.shape)
-
-
-def make_near(place, zed, other, halo):
-    square = jax.ShapeDtypeStruct((SLOTS, SLOTS), F32)
+def row_sums(rows, out):
+    wide = lane_sums(rows[:, :CHUNK].astype(F32))
+    for k in range(1, NCHUNK):
+        wide = wide + lane_sums(rows[:, k * CHUNK : (k + 1) * CHUNK].astype(F32))
+    out[...] = jnp.broadcast_to(jnp.sum(wide, axis=1, keepdims=True), out.shape)
+
+
+def edge_kernel(core, zed, halo, mine, theirs, zsum):
+    def products(half):
+        mine[...] = times(half, halo[...])
+        theirs[...] = times(halo[...], half).astype(BF16)
+
+    pl.when(core[0] == 0)(lambda: products(zed[:, HOURS // 2 :]))
+    pl.when(core[0] != 0)(lambda: products(zed[:, : HOURS // 2]))
+    row_sums(zed, zsum)
+
+
+def make_edge(place, zed, halo):
+    return pl.pallas_call(
+        edge_kernel,
+        in_specs=[SMEM, VMEM, VMEM],
+        out_specs=[VMEM] * 3,
+        out_shape=[shape(SLOTS, SLOTS), jax.ShapeDtypeStruct((SLOTS, SLOTS), BF16), shape(SLOTS, 128)],
+        compiler_params=params(16),
+        cost_estimate=pl.CostEstimate(flops=1 << 29, bytes_accessed=4 << 20, transcendentals=0),
+        name="edge_products",
+    )(place, zed, halo)
+
+
+def near_kernel(core, zed, other, mine, got, near, osum, held):
+    at = pl.multiple_of(core[0] * SLOTS, SLOTS)
+    near[:, pl.ds(at, SLOTS)] = (mine[...] + got[...].astype(F32)) * (1.0 / HOURS)
+    near[:, pl.ds(SLOTS - at, SLOTS)] = times(zed[...], other[...]) * (1.0 / HOURS)
+    row_sums(other, osum)
+    held[...] = other[...]
+
+
+def make_near(place, zed, other, mine, got):
     return pl.pallas_call(
         near_kernel,
-        in_specs=[SMEM, VMEM, VMEM, VMEM],
-        out_specs=[VMEM] * 5,
-        out_shape=[square] * 3 + [jax.ShapeDtypeStruct((SLOTS, 128), F32)] * 2,
-        scratch_shapes=[pltpu.VMEM((SLOTS, 128), F32)],
+        in_specs=[SMEM] + [VMEM] * 4,
+        out_specs=[VMEM] * 3,
+        out_shape=[
+            shape(SLOTS, 2 * SLOTS),
+            shape(SLOTS, 128),
+            jax.ShapeDtypeStruct((SLOTS, HOURS), BF16),
+        ],
         compiler_params=params(16),
-        cost_estimate=pl.CostEstimate(flops=1_073_741_824, bytes_accessed=6 << 20, transcendentals=0),
+        cost_estimate=pl.CostEstimate(flops=1 << 29, bytes_accessed=5 << 20, transcendentals=0),
         name="neighbour_correlation",
-    )(place, zed, other, halo)
-
-
-def near_sum_kernel(core, same, mine, got, near):
-    at = pl.multiple_of(core[0] * SLOTS, SLOTS)
-    near[:, pl.ds(at, SLOTS)] = (mine[...] + got[...]) * (1.0 / HOURS)
-    near[:, pl.ds(SLOTS - at, SLOTS)] = same[...]
-
-
-def near_sum(place, same, mine, got):
-    return pl.pallas_call(
-        near_sum_kernel,
-        in_specs=[SMEM, VMEM, VMEM, VMEM],
-        out_specs=VMEM,
-        out_shape=jax.ShapeDtypeStruct((SLOTS, 2 * SLOTS), F32),
-        compiler_params=params(8),
-        cost_estimate=pl.CostEstimate(flops=1 << 18, bytes_accessed=5 << 18, transcendentals=0),
-        name="neighbour_sum",
-    )(place, same, mine, got)
+    )(place, zed, other, mine, got)
 
 
 COMPS = 8 * HALF
@@ -179,7 +178,7 @@
             add(slice(k * CHUNK, (k + 1) * CHUNK), rows, k == 0)
 
 
-def late_kernel(here, place, far_a, far_b, zed, zsum, acc, *refs):
+def late_kernel(here, place, far, zed, zsum, acc, *refs):
     core, at = place[0], place[1]
     last = slice(COMPS - HALF, COMPS)
     if here:
@@ -190,7 +189,7 @@
 
     @pl.when(core == 0)
     def _():
-        rows = jnp.concatenate([far_a[...], far_b[...]], axis=0).reshape(COMPS, CHUNK)
+        rows = whole(far)
         out[...] = acc[...] + times(zed[:, hours_of(at, 4)], rows)
         if here:
             wide = rows.astype(F32)
@@ -202,7 +201,7 @@
         total = jnp.zeros((SLOTS, 128), F32)
         wide_1 = wide_2 = jnp.zeros((HALF, 128), F32)
         for k in range(NCHUNK):
-            rows = far_a[k] if k < 4 else far_b[k - 4]
+            rows = far[k]
             total = total + times(zed[:, k * CHUNK : (k + 1) * CHUNK], jnp.concatenate([rows, rows], axis=0))
             if here:
                 wide = rows.astype(F32)
@@ -241,47 +240,76 @@
     )(place, *blocks, zed, other)
 
 
-def make_late(place, blocks, zed, zsum, acc, sums=None, stats=None):
+def make_late(place, far, zed, zsum, acc, sums=None, stats=None):
     here = stats is None
     scratch = [pltpu.VMEM((COMPS, 128), F32)] * 2 if here else []
     extra = list(sums) if here else [stats]
     return pl.pallas_call(
         functools.partial(late_kernel, here),
-        in_specs=[SMEM] + [VMEM] * (5 + len(extra)),
+        in_specs=[SMEM] + [VMEM] * (4 + len(extra)),
         out_specs=[VMEM] * (2 if here else 1),
         out_shape=[shape(SLOTS, COMPS)] + ([shape(16, COMPS)] if here else []),
         scratch_shapes=scratch,
         compiler_params=params(24),
         cost_estimate=pl.CostEstimate(flops=1 << 27, bytes_accessed=4 << 20, transcendentals=0),
         name="late_composites",
-    )(place, *blocks, zed, zsum, acc, *extra)
-
-
-def merge_kernel(place, mine, got, out):
-    core, z, step = place[0], place[2], pl.program_id(0)
-    first = lax.broadcasted_iota(jnp.int32, (SLOTS, 128), 1) < HALF
-    tile = pl.ds(pl.multiple_of(step * 128, 128), 128)
-    low = jnp.where(core == 0, mine[:, tile], got[:, tile])
-    for odd in range(2):
-        d = (2 * step + odd - z) & 7
-        slot = jnp.where(d == 0, 0, jnp.where(d == 4, 7, jnp.where(d < 4, 2 * d, 15 - 2 * d)))
-        tile = pl.ds(pl.multiple_of((slot >> 1) * 128, 128), 128)
-        rows = jnp.where(core == 0, got[:, tile], mine[:, tile])
-        high = jnp.where((slot & 1) == 1, rows, pltpu.roll(rows, HALF, 1))
-        out[:, odd * 128 : odd * 128 + 128] = jnp.where(first, pltpu.roll(low, HALF, 1) if odd else low, high)
+    )(place, far, zed, zsum, acc, *extra)
+
+
+def merge_kernel(place, mine, got, out, held, sems):
+    core, z = place[0], place[2]
+    first = lax.broadcasted_iota(jnp.int32, (MERGE, 128), 1) < HALF
+    copies = []
+    for r in range(SLOTS // MERGE):
+        rows = slice(r * MERGE, (r + 1) * MERGE)
+        for to in range(8):
+            tile = slice(to // 2 * 128, to // 2 * 128 + 128)
+            low = jnp.where(core == 0, mine[rows, tile], got[rows, tile])
+            d = (to - z) & 7
+            slot = jnp.where(d == 0, 0, jnp.where(d == 4, 7, jnp.where(d < 4, 2 * d, 15 - 2 * d)))
+            tile = pl.ds(pl.multiple_of((slot >> 1) * 128, 128), 128)
+            high = jnp.where(core == 0, got[rows, tile], mine[rows, tile])
+            high = jnp.where((slot & 1) == 1, high, pltpu.roll(high, HALF, 1))
+            low = pltpu.roll(low, HALF, 1) if to % 2 else low
+            held[rows, to * 128 : to * 128 + 128] = jnp.where(first, low, high)
+        copies.append(pltpu.make_async_copy(held.at[rows], out.at[rows], sems.at[r]))
+        copies[-1].start()
+    for copy in copies:
+        copy.wait()
 
 
 def merge(place, mine, got):
     return pl.pallas_call(
         merge_kernel,
-        grid=(4,),
         in_specs=[SMEM, VMEM, VMEM],
-        out_specs=pl.BlockSpec((SLOTS, 256), lambda i: (0, i)),
+        out_specs=pl.BlockSpec(memory_space=pl.ANY),
         out_shape=shape(SLOTS, 1024),
+        scratch_shapes=[pltpu.VMEM((SLOTS, 1024), F32), pltpu.SemaphoreType.DMA((SLOTS // MERGE,))],
         compiler_params=params(8),
         cost_estimate=pl.CostEstimate(flops=1 << 20, bytes_accessed=2 << 20, transcendentals=0),
         name="merge_halves",
     )(place, mine, got)
+
+
+def spread_kernel(blocks, out):
+    total = blocks[0].astype(F32)
+    for i in range(1, 32):
+        total = total + blocks[i].astype(F32)
+    rows = total.astype(BF16)
+    for i in range(32):
+        out[i] = rows
+
+
+def sum_and_spread(blocks):
+    return pl.pallas_call(
+        spread_kernel,
+        in_specs=[VMEM],
+        out_specs=VMEM,
+        out_shape=jax.ShapeDtypeStruct(blocks.shape, BF16),
+        compiler_params=params(8),
+        cost_estimate=pl.CostEstimate(flops=1 << 18, bytes_accessed=1 << 20, transcendentals=0),
+        name="sum_and_spread",
+    )(blocks)
 
 
 def groups_and_rings():
@@ -309,30 +337,31 @@
 
     got = lax.ppermute(theirs, "c", swap)
     part = (own + got.astype(F32)).astype(BF16).reshape(32, 16, CHUNK)
-    part, zed, edge = together((part, zed, edge))
-    blocks = lax.all_to_all(part, ("y", "x"), split_axis=0, concat_axis=0, tiled=True)
-    block = jnp.sum(blocks.astype(F32), axis=0).astype(BF16)
-
+    part, edge = together((part, edge))
     across = [(i, i + 1) for i in range(1, 63, 2)]
     across += [(j, i) for i, j in across]
+    halo = lax.ppermute(edge, every[1:], across)
+    blocks = lax.all_to_all(part, ("y", "x"), split_axis=0, concat_axis=0, tiled=True)
+    spread = sum_and_spread(blocks)
+
+    near_mine, near_theirs, zsum = make_edge(place, zed, halo)
+    near_theirs, zed = together((near_theirs, zed))
+    near_got = lax.ppermute(near_theirs, every[1:], across)
     other = lax.ppermute(zed, "c", swap)
-    halo = lax.ppermute(edge, every[1:], across)
-    same, near_mine, near_theirs, zsum, osum = make_near(place, zed, other, halo)
-    near_got = lax.ppermute(near_theirs, every[1:], across)
-
-    spread = jnp.broadcast_to(block, (32, 16, CHUNK))
     first = lax.all_to_all(spread, every, split_axis=0, concat_axis=0, axis_index_groups=groups, tiled=True)
     first, near_got = together((first.reshape(8, HALF, CHUNK), near_got))
-    before, after = [first], [first]
+
+    above, below = [first], [first]
     for step in range(3):
-        before.append(lax.ppermute(before[step], every, up))
-        after.append(lax.ppermute(after[step], every, down))
-    far = [lax.ppermute(before[3][:4], every, up), lax.ppermute(after[3][4:], every, down)]
-
-    near_corr = near_sum(place, same, near_mine, near_got)
-    near_blocks = [first, before[1], after[1], before[2], after[2], before[3], after[3]]
-    early = make_early(place, near_blocks, zed, other)
-    far[0], near_corr = together((far[0], near_corr))
+        if step == 2:
+            near_corr, osum, other = make_near(place, zed, other, near_mine, near_got)
+            below[2], near_corr = together((below[2], near_corr))
+        above.append(lax.ppermute(above[step], every, up))
+        below.append(lax.ppermute(below[step], every, down))
+    far = lax.ppermute(above[3], every, up)
+
+    blocks = [first, above[1], below[1], above[2], below[2], above[3], below[3]]
+    early = make_early(place, blocks, zed, other)
     for_other, stats = make_late(place, far, other, osum, early[1], sums=early[2:])
     back = lax.ppermute(for_other, "c", swap)
     (mine,) = make_late(place, far, zed, zsum, early[0], stats=stats)

time: 130 us -> 125 us (0.962)
  local copies, waits for them, and re-layouts: 3.82 us -> 0.69 us
  Pallas kernels: 20.8 us -> 19 us
  starting transfers between devices: 68.2 us -> 66.7 us
    ppermute x1, starting transfers between devices: 12.9 us -> 3.32 us  [per_device(): near_got = lax.ppermute(near_theirs, every[1:], across)]
    ppermute x1, starting transfers between devices: 2.27 us -> 11.8 us  [per_device(): other = lax.ppermute(zed, 'c', swap)]
    ppermute x8 -> x7, starting transfers between devices: 25.9 us -> 21.3 us  [the longest x3 11.4 us: per_device(): below.append(lax.ppermute(below[step], every, down))]
    ppermute x1, starting transfers between devices: 5.33 us -> 8.15 us  [per_device(): back = lax.ppermute(for_other, 'c', swap)]
    ppermute x8 -> x7, waiting for transfers between devices: 14.8 us -> 17.6 us  [the longest x3 11.4 us: per_device(): above.append(lax.ppermute(above[step], every, up))]
    unnamed x8 -> x4, local copies, waits for them, and re-layouts: 2.93 us -> 0.69 us
    ppermute x1, waiting for transfers between devices: 4.89 us -> 3.37 us  [per_device(): near_got = lax.ppermute(near_theirs, every[1:], across)]
    pallas_call x3 -> x4, Pallas kernels: 8.05 us -> 8.37 us  [the longest x1 3.34 us: make_near(): pl.pallas_call(near_kernel, in_specs=[SMEM] + [VMEM] * 4, out_specs=[VMEM...]
  transfers between devices with their start and end apart: 15 -> 14, of which waited for: 7 -> 9; matrix products, arithmetic and copies ran while one was open for 1% -> 0% of each run, Pallas kernels for 9% -> 9%
where the time goes in v2:
time: 125 us; the launch traced here: 124 us
  starting transfers between devices  66.7 us (53%)
  waiting for transfers between devices  35.2 us (28%)
  Pallas kernels  19 us (15%)
  between operations  1.46 us (1%)
    all_to_all x1, waiting for transfers between devices, per_device(): lax.all_to_all(part, ('y', 'x'), split_axis=0, concat_axis=0, tiled=True)  12.6 us
    ppermute x1, starting transfers between devices, per_device(): other = lax.ppermute(zed, 'c', swap)  11.8 us
    ppermute x3, starting transfers between devices, per_device(): below.append(lax.ppermute(below[step], every, down))  11.4 us
    ppermute x3, waiting for transfers between devices, per_device(): above.append(lax.ppermute(above[step], every, up))  11.4 us
    ppermute x1, starting transfers between devices, per_device(): got = lax.ppermute(theirs, 'c', swap)  8.79 us
    ppermute x1, starting transfers between devices, per_device(): back = lax.ppermute(for_other, 'c', swap)  8.15 us
    ppermute x3, starting transfers between devices, per_device(): above.append(lax.ppermute(above[step], every, up))  8 us
    all_to_all x1, starting transfers between devices, per_device(): lax.all_to_all(spread, every, split_axis=0, concat_axis=0, axis_index_gro...  4.98 us
  transfers between devices with their start and end apart: 14, of which 9 were waited for; matrix products, arithmetic and copies ran while one was open for 0% of the time, Pallas kernels for 9%

profile of v2, /device:TPU:1, one launch (start us, length us, event | category | flops | bytes accessed | tf_op | source)
XLA Modules:
  0.0 124.0 jit_solution(1639315944330206436)
XLA Ops:
  1.3 0.1 pad_add_fusion.core.place
  1.4 0.0 copy-start
  1.4 0.7 copy-done
  2.0 4.6 %normalize_and_sum.1 = (bf16[256,4096]{1,0:T(8,128)(2,1)S(1)}, bf16[256,2048]{1,0:T(8,128)(2,1)S(1)}, f32[8,64,512]{2,1,0:T(8,128)S(1)}, bf16[8,64,512]{2,1,0:T(8,128)(2,1)S(1)}) custom-call(s32[1]{0:T(128)S(6)} %copy.5.count, s32[3]{0:T(128)S(1)} %pad_add_fusion.core.place, s32[1,256]{1,0:T(1,128)S(1)} %bitcast.9, bf16[256,4096]{1,0:T(8,128)(2,1)} %x.1), custom_call_target="tpu_custom_call" | custom-call | flops 300000000 | bytes 6291456 | tf_op jit(solution)/shard_map/normalize_and_sum/pallas_call | solution.py:63
  6.7 0.0 copy-start.1
  6.7 8.8 %collective-permute-start = (bf16[8,64,512]{2,1,0:T(8,128)(2,1)S(1)}, bf16[8,64,512]{2,1,0:T(8,128)(2,1)S(1)}, u32[]{:S(2)}, u32[]{:S(2)}) collective-permute-start(bf16[8,64,512]{2,1,0:T(8,128)(2,1)S(1)} %get-tuple-element.27), channel_id=1, source_target_pairs={{0,1},{1,0},{2,3},{3,2},{4,5},{5,4},{6,7},{7,6},{8,9},{9,8},{10,11... | collective-permute-start | bytes 1572872 | tf_op jit(solution)/shard_map/ppermute | solution.py:338
  15.5 1.5 %collective-permute-done = bf16[8,64,512]{2,1,0:T(8,128)(2,1)S(1)} collective-permute-done((bf16[8,64,512]{2,1,0:T(8,128)(2,1)S(1)}, bf16[8,64,512]{2,1,0:T(8,128)(2,1)S(1)}, u32[]{:S(2)}, u32[]{:S(2)}) %collective-permute-start) | collective-permute-done | bytes 524320 | tf_op jit(solution)/shard_map/ppermute | solution.py:338
  17.0 1.0 add_convert_fusion
  18.0 0.0 copy-done.1
  18.0 4.3 %all-to-all-start = ((bf16[32,16,512]{2,1,0:T(8,128)(2,1)}), bf16[32,16,512]{2,1,0:T(8,128)(2,1)S(1)}, u32[]{:S(2)}, u32[]{:S(2)}) async-start(bf16[32,16,512]{2,1,0:T(8,128)(2,1)} %bitcast.4), calls=%async_computation | async-start | bytes 1048576 | tf_op jit(solution)/shard_map/all_to_all | solution.py:344
  22.3 4.0 %collective-permute-start.1 = (bf16[256,2048]{1,0:T(8,128)(2,1)}, bf16[256,2048]{1,0:T(8,128)(2,1)}, u32[]{:S(2)}, u32[]{:S(2)}) collective-permute-start(bf16[256,2048]{1,0:T(8,128)(2,1)} %copy-done.1), channel_id=1, source_target_pairs={{1,2},{3,4},{5,6},{7,8},{9,10},{11,12},{13,14},{15,16},{17,18},{19... | collective-permute-start | bytes 3145736 | tf_op jit(solution)/shard_map/ppermute | solution.py:343
  26.3 12.6 %all-to-all-done.blocks = bf16[32,16,512]{2,1,0:T(8,128)(2,1)S(1)} async-done(((bf16[32,16,512]{2,1,0:T(8,128)(2,1)}), bf16[32,16,512]{2,1,0:T(8,128)(2,1)S(1)}, u32[]{:S(2)}, u32[]{:S(2)}) %all-to-all-start) | async-done | bytes 524320 | tf_op jit(solution)/shard_map/all_to_all | solution.py:344
  38.8 0.9 sum_and_spread.1
  39.8 5.0 %all-to-all-start.1 = ((bf16[32,16,512]{2,1,0:T(8,128)(2,1)}), bf16[32,16,512]{2,1,0:T(8,128)(2,1)S(1)}, u32[]{:S(2)}, u32[]{:S(2)}) async-start(bf16[32,16,512]{2,1,0:T(8,128)(2,1)} %sum_and_spread.1), calls=%async_computation.1 | async-start | bytes 1048576 | tf_op jit(solution)/shard_map/all_to_all | solution.py:351
  44.7 0.0 collective-permute-done.1.halo
  44.8 2.4 %edge_products.1 = (f32[256,256]{1,0:T(8,128)S(1)}, bf16[256,256]{1,0:T(8,128)(2,1)S(1)}, f32[256,128]{1,0:T(8,128)S(1)}) custom-call(s32[3]{0:T(128)S(1)} %pad_add_fusion.core.place, bf16[256,4096]{1,0:T(8,128)(2,1)S(1)} %get-tuple-element.35.zed.refs_7_, bf16[256,2048]{1,0:T(8,128)(2,1)} %collective-permute-done.1.halo), custom_call_target="tpu_custom_call" | custom-call | flops 536870912 | bytes 4194304 | tf_op jit(solution)/shard_map/edge_products/pallas_call | solution.py:105
  47.1 11.8 %collective-permute-start.5 = (bf16[256,4096]{1,0:T(8,128)(2,1)S(1)}, bf16[256,4096]{1,0:T(8,128)(2,1)}, u32[]{:S(2)}, u32[]{:S(2)}) collective-permute-start(bf16[256,4096]{1,0:T(8,128)(2,1)S(1)} %get-tuple-element.35.zed.refs_7_), channel_id=1, source_target_pairs={{0,1},{1,0},{2,3},{3,2},{4,5},{5,4},{6,7},{7,6},{8,9},{9,8},{10,11... | collective-permute-start | bytes 6291464 | tf_op jit(solution)/shard_map/ppermute | solution.py:350
  58.9 3.3 %collective-permute-start.2 = (bf16[256,256]{1,0:T(8,128)(2,1)S(1)}, bf16[256,256]{1,0:T(8,128)(2,1)S(1)}, u32[]{:S(2)}, u32[]{:S(2)}) collective-permute-start(bf16[256,256]{1,0:T(8,128)(2,1)S(1)} %get-tuple-element.33), channel_id=1, source_target_pairs={{1,2},{3,4},{5,6},{7,8},{9,10},{11,12},{13,14},{15,16},{17,18},{19... | collective-permute-start | bytes 393224 | tf_op jit(solution)/shard_map/ppermute | solution.py:349
  62.3 3.4 %collective-permute-done.2.got = bf16[256,256]{1,0:T(8,128)(2,1)S(1)} collective-permute-done((bf16[256,256]{1,0:T(8,128)(2,1)S(1)}, bf16[256,256]{1,0:T(8,128)(2,1)S(1)}, u32[]{:S(2)}, u32[]{:S(2)}) %collective-permute-start.2) | collective-permute-done | bytes 131104 | tf_op jit(solution)/shard_map/ppermute | solution.py:349
  65.6 0.0 all-to-all-done.1
  65.6 3.7 %collective-permute-start.6 = (bf16[8,64,512]{2,1,0:T(8,128)(2,1)S(1)}, bf16[8,64,512]{2,1,0:T(8,128)(2,1)S(1)}, u32[]{:S(2)}, u32[]{:S(2)}) collective-permute-start(bf16[8,64,512]{2,1,0:T(8,128)(2,1)S(1)} %bitcast.6), channel_id=1, source_target_pairs={{0,8},{1,65},{2,10},{3,67},{4,12},{5,69},{6,14},{7,71},{8,16},{9,7... | collective-permute-start | bytes 1572872 | tf_op jit(solution)/shard_map/ppermute | solution.py:359
  69.3 2.8 %collective-permute-start.3 = (bf16[8,64,512]{2,1,0:T(8,128)(2,1)S(1)}, bf16[8,64,512]{2,1,0:T(8,128)(2,1)S(1)}, u32[]{:S(2)}, u32[]{:S(2)}) collective-permute-start(bf16[8,64,512]{2,1,0:T(8,128)(2,1)S(1)} %bitcast.7), channel_id=1, source_target_pairs={{8,0},{65,1},{10,2},{67,3},{12,4},{69,5},{14,6},{71,7},{16,8},{73,... | collective-permute-start | bytes 1572872 | tf_op jit(solution)/shard_map/ppermute | solution.py:360
  72.1 4.9 %collective-permute-done.6.refs_1_ = bf16[8,64,512]{2,1,0:T(8,128)(2,1)S(1)} collective-permute-done((bf16[8,64,512]{2,1,0:T(8,128)(2,1)S(1)}, bf16[8,64,512]{2,1,0:T(8,128)(2,1)S(1)}, u32[]{:S(2)}, u32[]{:S(2)}) %collective-permute-start.6) | collective-permute-done | bytes 524320 | tf_op jit(solution)/shard_map/ppermute | solution.py:359
  77.0 2.4 %collective-permute-start.7 = (bf16[8,64,512]{2,1,0:T(8,128)(2,1)S(1)}, bf16[8,64,512]{2,1,0:T(8,128)(2,1)S(1)}, u32[]{:S(2)}, u32[]{:S(2)}) collective-permute-start(bf16[8,64,512]{2,1,0:T(8,128)(2,1)S(1)} %collective-permute-done.6.refs_1_), channel_id=1, source_target_pairs={{0,8},{1,65},{2,10},{3,67},{4,12},{5,69},{6,14},{7,71},{8,16},{9,7... | collective-permute-start | bytes 1572872 | tf_op jit(solution)/shard_map/ppermute | solution.py:359
  79.5 0.0 collective-permute-done.3.refs_2_
  79.5 4.0 %collective-permute-start.4 = (bf16[8,64,512]{2,1,0:T(8,128)(2,1)S(1)}, bf16[8,64,512]{2,1,0:T(8,128)(2,1)S(1)}, u32[]{:S(2)}, u32[]{:S(2)}) collective-permute-start(bf16[8,64,512]{2,1,0:T(8,128)(2,1)S(1)} %collective-permute-done.3.refs_2_), channel_id=1, source_target_pairs={{8,0},{65,1},{10,2},{67,3},{12,4},{69,5},{14,6},{71,7},{16,8},{73,... | collective-permute-start | bytes 1572872 | tf_op jit(solution)/shard_map/ppermute | solution.py:360
  83.6 4.9 %collective-permute-done.7.refs_3_ = bf16[8,64,512]{2,1,0:T(8,128)(2,1)S(1)} collective-permute-done((bf16[8,64,512]{2,1,0:T(8,128)(2,1)S(1)}, bf16[8,64,512]{2,1,0:T(8,128)(2,1)S(1)}, u32[]{:S(2)}, u32[]{:S(2)}) %collective-permute-start.7) | collective-permute-done | bytes 524320 | tf_op jit(solution)/shard_map/ppermute | solution.py:359
  88.5 1.9 %collective-permute-start.8 = (bf16[8,64,512]{2,1,0:T(8,128)(2,1)S(1)}, bf16[8,64,512]{2,1,0:T(8,128)(2,1)S(1)}, u32[]{:S(2)}, u32[]{:S(2)}) collective-permute-start(bf16[8,64,512]{2,1,0:T(8,128)(2,1)S(1)} %collective-permute-done.7.refs_3_), channel_id=1, source_target_pairs={{0,8},{1,65},{2,10},{3,67},{4,12},{5,69},{6,14},{7,71},{8,16},{9,7... | collective-permute-start | bytes 1572872 | tf_op jit(solution)/shard_map/ppermute | solution.py:359
  90.4 0.0 collective-permute-done.5.other
  90.4 3.3 %neighbour_correlation.1 = (f32[256,512]{1,0:T(8,128)}, f32[256,128]{1,0:T(8,128)S(1)}, bf16[256,4096]{1,0:T(8,128)(2,1)S(1)}) custom-call(s32[3]{0:T(128)S(1)} %pad_add_fusion.core.place, bf16[256,4096]{1,0:T(8,128)(2,1)S(1)} %get-tuple-element.35.zed.refs_7_, bf16[256,4096]{1,0:T(8,128)(2,1)} %collective-permute-done.5.other, ...), custom_call_target="tpu_custom_call" | custom-call | flops 536870912 | bytes 5242880 | tf_op jit(solution)/shard_map/neighbour_correlation/pallas_call | solution.py:125
  93.7 0.0 collective-permute-done.4.refs_4_
  93.7 4.6 %collective-permute-start.10 = (bf16[8,64,512]{2,1,0:T(8,128)(2,1)S(1)}, bf16[8,64,512]{2,1,0:T(8,128)(2,1)S(1)}, u32[]{:S(2)}, u32[]{:S(2)}) collective-permute-start(bf16[8,64,512]{2,1,0:T(8,128)(2,1)S(1)} %collective-permute-done.4.refs_4_), channel_id=1, source_target_pairs={{8,0},{65,1},{10,2},{67,3},{12,4},{69,5},{14,6},{71,7},{16,8},{73,... | collective-permute-start | bytes 1572872 | tf_op jit(solution)/shard_map/ppermute | solution.py:360
  98.3 1.6 %collective-permute-done.8.refs_5_ = bf16[8,64,512]{2,1,0:T(8,128)(2,1)S(1)} collective-permute-done((bf16[8,64,512]{2,1,0:T(8,128)(2,1)S(1)}, bf16[8,64,512]{2,1,0:T(8,128)(2,1)S(1)}, u32[]{:S(2)}, u32[]{:S(2)}) %collective-permute-start.8) | collective-permute-done | bytes 524320 | tf_op jit(solution)/shard_map/ppermute | solution.py:359
  99.9 1.9 %collective-permute-start.9 = (bf16[8,64,512]{2,1,0:T(8,128)(2,1)S(1)}, bf16[8,64,512]{2,1,0:T(8,128)(2,1)S(1)}, u32[]{:S(2)}, u32[]{:S(2)}) collective-permute-start(bf16[8,64,512]{2,1,0:T(8,128)(2,1)S(1)} %collective-permute-done.8.refs_5_), channel_id=1, source_target_pairs={{0,8},{1,65},{2,10},{3,67},{4,12},{5,69},{6,14},{7,71},{8,16},{9,7... | collective-permute-start | bytes 1572872 | tf_op jit(solution)/shard_map/ppermute | solution.py:361
  101.8 2.6 %collective-permute-done.10.refs_6_ = bf16[8,64,512]{2,1,0:T(8,128)(2,1)S(1)} collective-permute-done((bf16[8,64,512]{2,1,0:T(8,128)(2,1)S(1)}, bf16[8,64,512]{2,1,0:T(8,128)(2,1)S(1)}, u32[]{:S(2)}, u32[]{:S(2)}) %collective-permute-start.10) | collective-permute-done | bytes 524320 | tf_op jit(solution)/shard_map/ppermute | solution.py:360
  104.4 3.1 %early_composites.1 = (f32[256,512]{1,0:T(8,128)S(1)}, f32[256,512]{1,0:T(8,128)S(1)}, f32[512,128]{1,0:T(8,128)S(1)}, f32[512,128]{1,0:T(8,128)S(1)}) custom-call(s32[3]{0:T(128)S(1)} %pad_add_fusion.core.place, bf16[8,64,512]{2,1,0:T(8,128)(2,1)S(1)} %bitcast.8, bf16[8,64,512]{2,1,0:T(8,128)(2,1)S(1)} %collective-permute-done.6.refs_1_, ...), custom_call_target="tpu_custom_call" | custom-call | flops 2013265920 | bytes 9437184 | tf_op jit(solution)/shard_map/early_composites/pallas_call | solution.py:232
  107.5 3.5 %collective-permute-done.9.far = bf16[8,64,512]{2,1,0:T(8,128)(2,1)S(1)} collective-permute-done((bf16[8,64,512]{2,1,0:T(8,128)(2,1)S(1)}, bf16[8,64,512]{2,1,0:T(8,128)(2,1)S(1)}, u32[]{:S(2)}, u32[]{:S(2)}) %collective-permute-start.9) | collective-permute-done | bytes 524320 | tf_op jit(solution)/shard_map/ppermute | solution.py:361
  111.0 1.6 %late_composites.2 = (f32[256,512]{1,0:T(8,128)S(1)}, f32[16,512]{1,0:T(8,128)S(1)}) custom-call(s32[3]{0:T(128)S(1)} %pad_add_fusion.core.place, bf16[8,64,512]{2,1,0:T(8,128)(2,1)S(1)} %collective-permute-done.9.far, bf16[256,4096]{1,0:T(8,128)(2,1)S(1)} %get-tuple-element.42.refs_8_.zed, f32[256,128]{1,0:T(8,128)S(1)} %get-tuple-element.44.zsum, ...), custom_call_target="tpu_custom_call" | custom-call | flops 134217728 | bytes 4194304 | tf_op jit(solution)/shard_map/late_composites/pallas_call | solution.py:247
  112.6 8.2 %collective-permute-start.11 = (f32[256,512]{1,0:T(8,128)S(1)}, f32[256,512]{1,0:T(8,128)S(1)}, u32[]{:S(2)}, u32[]{:S(2)}) collective-permute-start(f32[256,512]{1,0:T(8,128)S(1)} %get-tuple-element.49), channel_id=1, source_target_pairs={{0,1},{1,0},{2,3},{3,2},{4,5},{5,4},{6,7},{7,6},{8,9},{9,8},{10,11... | collective-permute-start | bytes 1572872 | tf_op jit(solution)/shard_map/ppermute | solution.py:366
  120.7 1.4 %late_composites.3.mine = f32[256,512]{1,0:T(8,128)S(1)} custom-call(s32[3]{0:T(128)S(1)} %pad_add_fusion.core.place, bf16[8,64,512]{2,1,0:T(8,128)(2,1)S(1)} %collective-permute-done.9.far, bf16[256,4096]{1,0:T(8,128)(2,1)S(1)} %get-tuple-element.35.zed.refs_7_, f32[256,128]{1,0:T(8,128)S(1)} %get-tuple-element.40.zsum, ...), custom_call_target="tpu_custom_call" | custom-call | flops 134217728 | bytes 4194304 | tf_op jit(solution)/shard_map/late_composites/pallas_call | solution.py:247
  122.1 0.1 collective-permute-done.11.got
  122.3 1.8 %merge_halves.1 = f32[256,1024]{1,0:T(8,128)} custom-call(s32[3]{0:T(128)S(1)} %pad_add_fusion.core.place, f32[256,512]{1,0:T(8,128)S(1)} %late_composites.3.mine, f32[256,512]{1,0:T(8,128)S(1)} %collective-permute-done.11.got), custom_call_target="tpu_custom_call" | custom-call | flops 1048576 | bytes 2097152 | tf_op jit(solution)/shard_map/merge_halves/pallas_call | solution.py:282
Async XLA Ops:
  1.4 0.7 copy-start
  6.7 11.3 %copy-start.1 = (bf16[256,2048]{1,0:T(8,128)(2,1)}, bf16[256,2048]{1,0:T(8,128)(2,1)S(1)}, u32[]{:S(2)}) copy-start(bf16[256,2048]{1,0:T(8,128)(2,1)S(1)} %get-tuple-element.31) | copy-start | bytes 3145732
  6.7 10.3 %collective-permute-start = (bf16[8,64,512]{2,1,0:T(8,128)(2,1)S(1)}, bf16[8,64,512]{2,1,0:T(8,128)(2,1)S(1)}, u32[]{:S(2)}, u32[]{:S(2)}) collective-permute-start(bf16[8,64,512]{2,1,0:T(8,128)(2,1)S(1)} %get-tuple-element.27), channel_id=1, source_target_pairs={{0,1},{1,0},{2,3},{3,2},{4,5},{5,4},{6,7},{7,6},{8,9},{9,8},{10,11... | collective-permute-start | bytes 1572872 | tf_op jit(solution)/shard_map/ppermute | solution.py:338
  18.0 20.9 %all-to-all-start = ((bf16[32,16,512]{2,1,0:T(8,128)(2,1)}), bf16[32,16,512]{2,1,0:T(8,128)(2,1)S(1)}, u32[]{:S(2)}, u32[]{:S(2)}) async-start(bf16[32,16,512]{2,1,0:T(8,128)(2,1)} %bitcast.4), calls=%async_computation | async-start | bytes 1048576 | tf_op jit(solution)/shard_map/all_to_all | solution.py:344
  22.3 22.5 %collective-permute-start.1 = (bf16[256,2048]{1,0:T(8,128)(2,1)}, bf16[256,2048]{1,0:T(8,128)(2,1)}, u32[]{:S(2)}, u32[]{:S(2)}) collective-permute-start(bf16[256,2048]{1,0:T(8,128)(2,1)} %copy-done.1), channel_id=1, source_target_pairs={{1,2},{3,4},{5,6},{7,8},{9,10},{11,12},{13,14},{15,16},{17,18},{19... | collective-permute-start | bytes 3145736 | tf_op jit(solution)/shard_map/ppermute | solution.py:343
  39.8 25.9 %all-to-all-start.1 = ((bf16[32,16,512]{2,1,0:T(8,128)(2,1)}), bf16[32,16,512]{2,1,0:T(8,128)(2,1)S(1)}, u32[]{:S(2)}, u32[]{:S(2)}) async-start(bf16[32,16,512]{2,1,0:T(8,128)(2,1)} %sum_and_spread.1), calls=%async_computation.1 | async-start | bytes 1048576 | tf_op jit(solution)/shard_map/all_to_all | solution.py:351
  47.1 43.3 %collective-permute-start.5 = (bf16[256,4096]{1,0:T(8,128)(2,1)S(1)}, bf16[256,4096]{1,0:T(8,128)(2,1)}, u32[]{:S(2)}, u32[]{:S(2)}) collective-permute-start(bf16[256,4096]{1,0:T(8,128)(2,1)S(1)} %get-tuple-element.35.zed.refs_7_), channel_id=1, source_target_pairs={{0,1},{1,0},{2,3},{3,2},{4,5},{5,4},{6,7},{7,6},{8,9},{9,8},{10,11... | collective-permute-start | bytes 6291464 | tf_op jit(solution)/shard_map/ppermute | solution.py:350
  58.9 6.7 %collective-permute-start.2 = (bf16[256,256]{1,0:T(8,128)(2,1)S(1)}, bf16[256,256]{1,0:T(8,128)(2,1)S(1)}, u32[]{:S(2)}, u32[]{:S(2)}) collective-permute-start(bf16[256,256]{1,0:T(8,128)(2,1)S(1)} %get-tuple-element.33), channel_id=1, source_target_pairs={{1,2},{3,4},{5,6},{7,8},{9,10},{11,12},{13,14},{15,16},{17,18},{19... | collective-permute-start | bytes 393224 | tf_op jit(solution)/shard_map/ppermute | solution.py:349
  65.6 11.4 %collective-permute-start.6 = (bf16[8,64,512]{2,1,0:T(8,128)(2,1)S(1)}, bf16[8,64,512]{2,1,0:T(8,128)(2,1)S(1)}, u32[]{:S(2)}, u32[]{:S(2)}) collective-permute-start(bf16[8,64,512]{2,1,0:T(8,128)(2,1)S(1)} %bitcast.6), channel_id=1, source_target_pairs={{0,8},{1,65},{2,10},{3,67},{4,12},{5,69},{6,14},{7,71},{8,16},{9,7... | collective-permute-start | bytes 1572872 | tf_op jit(solution)/shard_map/ppermute | solution.py:359
  69.3 10.2 %collective-permute-start.3 = (bf16[8,64,512]{2,1,0:T(8,128)(2,1)S(1)}, bf16[8,64,512]{2,1,0:T(8,128)(2,1)S(1)}, u32[]{:S(2)}, u32[]{:S(2)}) collective-permute-start(bf16[8,64,512]{2,1,0:T(8,128)(2,1)S(1)} %bitcast.7), channel_id=1, source_target_pairs={{8,0},{65,1},{10,2},{67,3},{12,4},{69,5},{14,6},{71,7},{16,8},{73,... | collective-permute-start | bytes 1572872 | tf_op jit(solution)/shard_map/ppermute | solution.py:360
  77.0 11.4 %collective-permute-start.7 = (bf16[8,64,512]{2,1,0:T(8,128)(2,1)S(1)}, bf16[8,64,512]{2,1,0:T(8,128)(2,1)S(1)}, u32[]{:S(2)}, u32[]{:S(2)}) collective-permute-start(bf16[8,64,512]{2,1,0:T(8,128)(2,1)S(1)} %collective-permute-done.6.refs_1_), channel_id=1, source_target_pairs={{0,8},{1,65},{2,10},{3,67},{4,12},{5,69},{6,14},{7,71},{8,16},{9,7... | collective-permute-start | bytes 1572872 | tf_op jit(solution)/shard_map/ppermute | solution.py:359
  79.5 14.2 %collective-permute-start.4 = (bf16[8,64,512]{2,1,0:T(8,128)(2,1)S(1)}, bf16[8,64,512]{2,1,0:T(8,128)(2,1)S(1)}, u32[]{:S(2)}, u32[]{:S(2)}) collective-permute-start(bf16[8,64,512]{2,1,0:T(8,128)(2,1)S(1)} %collective-permute-done.3.refs_2_), channel_id=1, source_target_pairs={{8,0},{65,1},{10,2},{67,3},{12,4},{69,5},{14,6},{71,7},{16,8},{73,... | collective-permute-start | bytes 1572872 | tf_op jit(solution)/shard_map/ppermute | solution.py:360
  88.5 11.4 %collective-permute-start.8 = (bf16[8,64,512]{2,1,0:T(8,128)(2,1)S(1)}, bf16[8,64,512]{2,1,0:T(8,128)(2,1)S(1)}, u32[]{:S(2)}, u32[]{:S(2)}) collective-permute-start(bf16[8,64,512]{2,1,0:T(8,128)(2,1)S(1)} %collective-permute-done.7.refs_3_), channel_id=1, source_target_pairs={{0,8},{1,65},{2,10},{3,67},{4,12},{5,69},{6,14},{7,71},{8,16},{9,7... | collective-permute-start | bytes 1572872 | tf_op jit(solution)/shard_map/ppermute | solution.py:359
  93.7 10.7 %collective-permute-start.10 = (bf16[8,64,512]{2,1,0:T(8,128)(2,1)S(1)}, bf16[8,64,512]{2,1,0:T(8,128)(2,1)S(1)}, u32[]{:S(2)}, u32[]{:S(2)}) collective-permute-start(bf16[8,64,512]{2,1,0:T(8,128)(2,1)S(1)} %collective-permute-done.4.refs_4_), channel_id=1, source_target_pairs={{8,0},{65,1},{10,2},{67,3},{12,4},{69,5},{14,6},{71,7},{16,8},{73,... | collective-permute-start | bytes 1572872 | tf_op jit(solution)/shard_map/ppermute | solution.py:360
  99.9 11.1 %collective-permute-start.9 = (bf16[8,64,512]{2,1,0:T(8,128)(2,1)S(1)}, bf16[8,64,512]{2,1,0:T(8,128)(2,1)S(1)}, u32[]{:S(2)}, u32[]{:S(2)}) collective-permute-start(bf16[8,64,512]{2,1,0:T(8,128)(2,1)S(1)} %collective-permute-done.8.refs_5_), channel_id=1, source_target_pairs={{0,8},{1,65},{2,10},{3,67},{4,12},{5,69},{6,14},{7,71},{8,16},{9,7... | collective-permute-start | bytes 1572872 | tf_op jit(solution)/shard_map/ppermute | solution.py:361
  112.6 9.7 %collective-permute-start.11 = (f32[256,512]{1,0:T(8,128)S(1)}, f32[256,512]{1,0:T(8,128)S(1)}, u32[]{:S(2)}, u32[]{:S(2)}) collective-permute-start(f32[256,512]{1,0:T(8,128)S(1)} %get-tuple-element.49), channel_id=1, source_target_pairs={{0,1},{1,0},{2,3},{3,2},{4,5},{5,4},{6,7},{7,6},{8,9},{9,8},{10,11... | collective-permute-start | bytes 1572872 | tf_op jit(solution)/shard_map/ppermute | solution.py:366

commit v3 on v2

--- a/solution.py
+++ b/solution.py
@@ -30,6 +30,13 @@
 HBM = pl.BlockSpec(memory_space=pltpu.HBM)
 
 
+def sum_of(pieces):
+    sums = pieces[:4]
+    for i, piece in enumerate(pieces[4:]):
+        sums[i % 4] = sums[i % 4] + piece
+    return (sums[0] + sums[1]) + (sums[2] + sums[3])
+
+
 def zed_kernel(count, core, ids, x, zed, edge, own, theirs, held, sems):
     steps = SLOTS // ROWS
     rows_of = lambda step: pl.ds(step * ROWS, ROWS)
@@ -40,14 +47,17 @@
         copy.start()
     for step, copy in enumerate(copies):
         copy.wait()
-        values = held[rows_of(step), :].astype(F32)
-        center = values - jnp.mean(values, axis=1, keepdims=True)
-        scale = lax.rsqrt(jnp.mean(center * center, axis=1, keepdims=True) + EPS)
+        pieces = [held[rows_of(step), k * 128 : k * 128 + 128].astype(F32) for k in range(HOURS // 128)]
+        mean = jnp.sum(sum_of(pieces), axis=1, keepdims=True) * (1.0 / HOURS)
+        squares = sum_of([jnp.square(piece - mean) for piece in pieces])
+        scale = lax.rsqrt(jnp.sum(squares, axis=1, keepdims=True) * (1.0 / HOURS) + EPS)
         slot = step * ROWS + lax.broadcasted_iota(jnp.int32, (ROWS, 1), 0)
-        live = (slot < count[0]).astype(F32)
-        rows = (center * scale * live).astype(BF16)
-        zed[rows_of(step), :] = rows
-        edge[rows_of(step), :] = jnp.where(core[0] == 0, rows[:, : HOURS // 2], rows[:, HOURS // 2 :])
+        scale = scale * (slot < count[0]).astype(F32)
+        for k in range(HOURS // 256):
+            early, late = (((pieces[i] - mean) * scale).astype(BF16) for i in (k, k + HOURS // 256))
+            zed[rows_of(step), k * 128 : k * 128 + 128] = early
+            zed[rows_of(step), HOURS // 2 + k * 128 : HOURS // 2 + k * 128 + 128] = late
+            edge[rows_of(step), k * 128 : k * 128 + 128] = jnp.where(core[0] == 0, early, late)
 
     index = lax.broadcasted_iota(jnp.int32, (COMP_REG, SLOTS), 0)
     index = (index + HALF * core[0]) & (COMP_REG - 1)

time: 125 us -> 124 us (level)
  no operation moved by 1% of the time
where the time goes in v3:
time: 124 us
  starting transfers between devices  66.7 us (54%)
  waiting for transfers between devices  35.2 us (28%)
  Pallas kernels  18.6 us (15%)
  between operations  1.46 us (1%)
    all_to_all x1, waiting for transfers between devices, per_device(): lax.all_to_all(part, ('y', 'x'), split_axis=0, concat_axis=0, tiled=True)  12.6 us
    ppermute x1, starting transfers between devices, per_device(): other = lax.ppermute(zed, 'c', swap)  11.8 us
    ppermute x3, starting transfers between devices, per_device(): below.append(lax.ppermute(below[step], every, down))  11.4 us
    ppermute x3, waiting for transfers between devices, per_device(): above.append(lax.ppermute(above[step], every, up))  11.4 us
    ppermute x1, starting transfers between devices, per_device(): got = lax.ppermute(theirs, 'c', swap)  8.78 us
    ppermute x1, starting transfers between devices, per_device(): back = lax.ppermute(for_other, 'c', swap)  8.15 us
    ppermute x3, starting transfers between devices, per_device(): above.append(lax.ppermute(above[step], every, up))  8 us
    all_to_all x1, starting transfers between devices, per_device(): lax.all_to_all(spread, every, split_axis=0, concat_axis=0, axis_index_gro...  4.98 us
  transfers between devices with their start and end apart: 14, of which 9 were waited for; matrix products, arithmetic and copies ran while one was open for 0% of the time, Pallas kernels for 9%

profile of v3, /device:TPU:1, one launch (start us, length us, event | category | flops | bytes accessed | tf_op | source)
XLA Modules:
  0.0 123.6 jit_solution(15141109675994028762)
XLA Ops:
  1.3 0.1 pad_add_fusion.core.place
  1.4 0.0 copy-start
  1.4 0.7 copy-done
  2.0 4.3 %normalize_and_sum.1 = (bf16[256,4096]{1,0:T(8,128)(2,1)S(1)}, bf16[256,2048]{1,0:T(8,128)(2,1)S(1)}, f32[8,64,512]{2,1,0:T(8,128)S(1)}, bf16[8,64,512]{2,1,0:T(8,128)(2,1)S(1)}) custom-call(s32[1]{0:T(128)S(6)} %copy.5.count, s32[3]{0:T(128)S(1)} %pad_add_fusion.core.place, s32[1,256]{1,0:T(1,128)S(1)} %bitcast.9, bf16[256,4096]{1,0:T(8,128)(2,1)} %x.1), custom_call_target="tpu_custom_call" | custom-call | flops 300000000 | bytes 6291456 | tf_op jit(solution)/shard_map/normalize_and_sum/pallas_call | solution.py:73
  6.3 0.0 copy-start.1
  6.3 8.8 %collective-permute-start = (bf16[8,64,512]{2,1,0:T(8,128)(2,1)S(1)}, bf16[8,64,512]{2,1,0:T(8,128)(2,1)S(1)}, u32[]{:S(2)}, u32[]{:S(2)}) collective-permute-start(bf16[8,64,512]{2,1,0:T(8,128)(2,1)S(1)} %get-tuple-element.27), channel_id=1, source_target_pairs={{0,1},{1,0},{2,3},{3,2},{4,5},{5,4},{6,7},{7,6},{8,9},{9,8},{10,11... | collective-permute-start | bytes 1572872 | tf_op jit(solution)/shard_map/ppermute | solution.py:348
  15.1 1.5 %collective-permute-done = bf16[8,64,512]{2,1,0:T(8,128)(2,1)S(1)} collective-permute-done((bf16[8,64,512]{2,1,0:T(8,128)(2,1)S(1)}, bf16[8,64,512]{2,1,0:T(8,128)(2,1)S(1)}, u32[]{:S(2)}, u32[]{:S(2)}) %collective-permute-start) | collective-permute-done | bytes 524320 | tf_op jit(solution)/shard_map/ppermute | solution.py:348
  16.6 1.0 add_convert_fusion
  17.6 0.0 copy-done.1
  17.6 4.3 %all-to-all-start = ((bf16[32,16,512]{2,1,0:T(8,128)(2,1)}), bf16[32,16,512]{2,1,0:T(8,128)(2,1)S(1)}, u32[]{:S(2)}, u32[]{:S(2)}) async-start(bf16[32,16,512]{2,1,0:T(8,128)(2,1)} %bitcast.4), calls=%async_computation | async-start | bytes 1048576 | tf_op jit(solution)/shard_map/all_to_all | solution.py:354
  21.9 4.0 %collective-permute-start.1 = (bf16[256,2048]{1,0:T(8,128)(2,1)}, bf16[256,2048]{1,0:T(8,128)(2,1)}, u32[]{:S(2)}, u32[]{:S(2)}) collective-permute-start(bf16[256,2048]{1,0:T(8,128)(2,1)} %copy-done.1), channel_id=1, source_target_pairs={{1,2},{3,4},{5,6},{7,8},{9,10},{11,12},{13,14},{15,16},{17,18},{19... | collective-permute-start | bytes 3145736 | tf_op jit(solution)/shard_map/ppermute | solution.py:353
  25.9 12.6 %all-to-all-done.blocks = bf16[32,16,512]{2,1,0:T(8,128)(2,1)S(1)} async-done(((bf16[32,16,512]{2,1,0:T(8,128)(2,1)}), bf16[32,16,512]{2,1,0:T(8,128)(2,1)S(1)}, u32[]{:S(2)}, u32[]{:S(2)}) %all-to-all-start) | async-done | bytes 524320 | tf_op jit(solution)/shard_map/all_to_all | solution.py:354
  38.5 0.9 sum_and_spread.1
  39.4 5.0 %all-to-all-start.1 = ((bf16[32,16,512]{2,1,0:T(8,128)(2,1)}), bf16[32,16,512]{2,1,0:T(8,128)(2,1)S(1)}, u32[]{:S(2)}, u32[]{:S(2)}) async-start(bf16[32,16,512]{2,1,0:T(8,128)(2,1)} %sum_and_spread.1), calls=%async_computation.1 | async-start | bytes 1048576 | tf_op jit(solution)/shard_map/all_to_all | solution.py:361
  44.4 0.0 collective-permute-done.1.halo
  44.4 2.3 %edge_products.1 = (f32[256,256]{1,0:T(8,128)S(1)}, bf16[256,256]{1,0:T(8,128)(2,1)S(1)}, f32[256,128]{1,0:T(8,128)S(1)}) custom-call(s32[3]{0:T(128)S(1)} %pad_add_fusion.core.place, bf16[256,4096]{1,0:T(8,128)(2,1)S(1)} %get-tuple-element.35.zed.refs_7_, bf16[256,2048]{1,0:T(8,128)(2,1)} %collective-permute-done.1.halo), custom_call_target="tpu_custom_call" | custom-call | flops 536870912 | bytes 4194304 | tf_op jit(solution)/shard_map/edge_products/pallas_call | solution.py:115
  46.7 11.8 %collective-permute-start.5 = (bf16[256,4096]{1,0:T(8,128)(2,1)S(1)}, bf16[256,4096]{1,0:T(8,128)(2,1)}, u32[]{:S(2)}, u32[]{:S(2)}) collective-permute-start(bf16[256,4096]{1,0:T(8,128)(2,1)S(1)} %get-tuple-element.35.zed.refs_7_), channel_id=1, source_target_pairs={{0,1},{1,0},{2,3},{3,2},{4,5},{5,4},{6,7},{7,6},{8,9},{9,8},{10,11... | collective-permute-start | bytes 6291464 | tf_op jit(solution)/shard_map/ppermute | solution.py:360
  58.5 3.3 %collective-permute-start.2 = (bf16[256,256]{1,0:T(8,128)(2,1)S(1)}, bf16[256,256]{1,0:T(8,128)(2,1)S(1)}, u32[]{:S(2)}, u32[]{:S(2)}) collective-permute-start(bf16[256,256]{1,0:T(8,128)(2,1)S(1)} %get-tuple-element.33), channel_id=1, source_target_pairs={{1,2},{3,4},{5,6},{7,8},{9,10},{11,12},{13,14},{15,16},{17,18},{19... | collective-permute-start | bytes 393224 | tf_op jit(solution)/shard_map/ppermute | solution.py:359
  61.9 3.4 %collective-permute-done.2.got = bf16[256,256]{1,0:T(8,128)(2,1)S(1)} collective-permute-done((bf16[256,256]{1,0:T(8,128)(2,1)S(1)}, bf16[256,256]{1,0:T(8,128)(2,1)S(1)}, u32[]{:S(2)}, u32[]{:S(2)}) %collective-permute-start.2) | collective-permute-done | bytes 131104 | tf_op jit(solution)/shard_map/ppermute | solution.py:359
  65.2 0.0 all-to-all-done.1
  65.2 3.6 %collective-permute-start.6 = (bf16[8,64,512]{2,1,0:T(8,128)(2,1)S(1)}, bf16[8,64,512]{2,1,0:T(8,128)(2,1)S(1)}, u32[]{:S(2)}, u32[]{:S(2)}) collective-permute-start(bf16[8,64,512]{2,1,0:T(8,128)(2,1)S(1)} %bitcast.6), channel_id=1, source_target_pairs={{0,8},{1,65},{2,10},{3,67},{4,12},{5,69},{6,14},{7,71},{8,16},{9,7... | collective-permute-start | bytes 1572872 | tf_op jit(solution)/shard_map/ppermute | solution.py:369
  68.9 2.8 %collective-permute-start.3 = (bf16[8,64,512]{2,1,0:T(8,128)(2,1)S(1)}, bf16[8,64,512]{2,1,0:T(8,128)(2,1)S(1)}, u32[]{:S(2)}, u32[]{:S(2)}) collective-permute-start(bf16[8,64,512]{2,1,0:T(8,128)(2,1)S(1)} %bitcast.7), channel_id=1, source_target_pairs={{8,0},{65,1},{10,2},{67,3},{12,4},{69,5},{14,6},{71,7},{16,8},{73,... | collective-permute-start | bytes 1572872 | tf_op jit(solution)/shard_map/ppermute | solution.py:370
  71.7 4.9 %collective-permute-done.6.refs_1_ = bf16[8,64,512]{2,1,0:T(8,128)(2,1)S(1)} collective-permute-done((bf16[8,64,512]{2,1,0:T(8,128)(2,1)S(1)}, bf16[8,64,512]{2,1,0:T(8,128)(2,1)S(1)}, u32[]{:S(2)}, u32[]{:S(2)}) %collective-permute-start.6) | collective-permute-done | bytes 524320 | tf_op jit(solution)/shard_map/ppermute | solution.py:369
  76.7 2.4 %collective-permute-start.7 = (bf16[8,64,512]{2,1,0:T(8,128)(2,1)S(1)}, bf16[8,64,512]{2,1,0:T(8,128)(2,1)S(1)}, u32[]{:S(2)}, u32[]{:S(2)}) collective-permute-start(bf16[8,64,512]{2,1,0:T(8,128)(2,1)S(1)} %collective-permute-done.6.refs_1_), channel_id=1, source_target_pairs={{0,8},{1,65},{2,10},{3,67},{4,12},{5,69},{6,14},{7,71},{8,16},{9,7... | collective-permute-start | bytes 1572872 | tf_op jit(solution)/shard_map/ppermute | solution.py:369
  79.1 0.0 collective-permute-done.3.refs_2_
  79.1 4.0 %collective-permute-start.4 = (bf16[8,64,512]{2,1,0:T(8,128)(2,1)S(1)}, bf16[8,64,512]{2,1,0:T(8,128)(2,1)S(1)}, u32[]{:S(2)}, u32[]{:S(2)}) collective-permute-start(bf16[8,64,512]{2,1,0:T(8,128)(2,1)S(1)} %collective-permute-done.3.refs_2_), channel_id=1, source_target_pairs={{8,0},{65,1},{10,2},{67,3},{12,4},{69,5},{14,6},{71,7},{16,8},{73,... | collective-permute-start | bytes 1572872 | tf_op jit(solution)/shard_map/ppermute | solution.py:370
  83.2 4.9 %collective-permute-done.7.refs_3_ = bf16[8,64,512]{2,1,0:T(8,128)(2,1)S(1)} collective-permute-done((bf16[8,64,512]{2,1,0:T(8,128)(2,1)S(1)}, bf16[8,64,512]{2,1,0:T(8,128)(2,1)S(1)}, u32[]{:S(2)}, u32[]{:S(2)}) %collective-permute-start.7) | collective-permute-done | bytes 524320 | tf_op jit(solution)/shard_map/ppermute | solution.py:369
  88.1 1.9 %collective-permute-start.8 = (bf16[8,64,512]{2,1,0:T(8,128)(2,1)S(1)}, bf16[8,64,512]{2,1,0:T(8,128)(2,1)S(1)}, u32[]{:S(2)}, u32[]{:S(2)}) collective-permute-start(bf16[8,64,512]{2,1,0:T(8,128)(2,1)S(1)} %collective-permute-done.7.refs_3_), channel_id=1, source_target_pairs={{0,8},{1,65},{2,10},{3,67},{4,12},{5,69},{6,14},{7,71},{8,16},{9,7... | collective-permute-start | bytes 1572872 | tf_op jit(solution)/shard_map/ppermute | solution.py:369
  90.0 0.0 collective-permute-done.5.other
  90.0 3.3 %neighbour_correlation.1 = (f32[256,512]{1,0:T(8,128)}, f32[256,128]{1,0:T(8,128)S(1)}, bf16[256,4096]{1,0:T(8,128)(2,1)S(1)}) custom-call(s32[3]{0:T(128)S(1)} %pad_add_fusion.core.place, bf16[256,4096]{1,0:T(8,128)(2,1)S(1)} %get-tuple-element.35.zed.refs_7_, bf16[256,4096]{1,0:T(8,128)(2,1)} %collective-permute-done.5.other, ...), custom_call_target="tpu_custom_call" | custom-call | flops 536870912 | bytes 5242880 | tf_op jit(solution)/shard_map/neighbour_correlation/pallas_call | solution.py:135
  93.3 0.0 collective-permute-done.4.refs_4_
  93.3 4.6 %collective-permute-start.10 = (bf16[8,64,512]{2,1,0:T(8,128)(2,1)S(1)}, bf16[8,64,512]{2,1,0:T(8,128)(2,1)S(1)}, u32[]{:S(2)}, u32[]{:S(2)}) collective-permute-start(bf16[8,64,512]{2,1,0:T(8,128)(2,1)S(1)} %collective-permute-done.4.refs_4_), channel_id=1, source_target_pairs={{8,0},{65,1},{10,2},{67,3},{12,4},{69,5},{14,6},{71,7},{16,8},{73,... | collective-permute-start | bytes 1572872 | tf_op jit(solution)/shard_map/ppermute | solution.py:370
  97.9 1.6 %collective-permute-done.8.refs_5_ = bf16[8,64,512]{2,1,0:T(8,128)(2,1)S(1)} collective-permute-done((bf16[8,64,512]{2,1,0:T(8,128)(2,1)S(1)}, bf16[8,64,512]{2,1,0:T(8,128)(2,1)S(1)}, u32[]{:S(2)}, u32[]{:S(2)}) %collective-permute-start.8) | collective-permute-done | bytes 524320 | tf_op jit(solution)/shard_map/ppermute | solution.py:369
  99.5 1.9 %collective-permute-start.9 = (bf16[8,64,512]{2,1,0:T(8,128)(2,1)S(1)}, bf16[8,64,512]{2,1,0:T(8,128)(2,1)S(1)}, u32[]{:S(2)}, u32[]{:S(2)}) collective-permute-start(bf16[8,64,512]{2,1,0:T(8,128)(2,1)S(1)} %collective-permute-done.8.refs_5_), channel_id=1, source_target_pairs={{0,8},{1,65},{2,10},{3,67},{4,12},{5,69},{6,14},{7,71},{8,16},{9,7... | collective-permute-start | bytes 1572872 | tf_op jit(solution)/shard_map/ppermute | solution.py:371
  101.4 2.6 %collective-permute-done.10.refs_6_ = bf16[8,64,512]{2,1,0:T(8,128)(2,1)S(1)} collective-permute-done((bf16[8,64,512]{2,1,0:T(8,128)(2,1)S(1)}, bf16[8,64,512]{2,1,0:T(8,128)(2,1)S(1)}, u32[]{:S(2)}, u32[]{:S(2)}) %collective-permute-start.10) | collective-permute-done | bytes 524320 | tf_op jit(solution)/shard_map/ppermute | solution.py:370
  104.0 3.1 %early_composites.1 = (f32[256,512]{1,0:T(8,128)S(1)}, f32[256,512]{1,0:T(8,128)S(1)}, f32[512,128]{1,0:T(8,128)S(1)}, f32[512,128]{1,0:T(8,128)S(1)}) custom-call(s32[3]{0:T(128)S(1)} %pad_add_fusion.core.place, bf16[8,64,512]{2,1,0:T(8,128)(2,1)S(1)} %bitcast.8, bf16[8,64,512]{2,1,0:T(8,128)(2,1)S(1)} %collective-permute-done.6.refs_1_, ...), custom_call_target="tpu_custom_call" | custom-call | flops 2013265920 | bytes 9437184 | tf_op jit(solution)/shard_map/early_composites/pallas_call | solution.py:242
  107.1 3.5 %collective-permute-done.9.far = bf16[8,64,512]{2,1,0:T(8,128)(2,1)S(1)} collective-permute-done((bf16[8,64,512]{2,1,0:T(8,128)(2,1)S(1)}, bf16[8,64,512]{2,1,0:T(8,128)(2,1)S(1)}, u32[]{:S(2)}, u32[]{:S(2)}) %collective-permute-start.9) | collective-permute-done | bytes 524320 | tf_op jit(solution)/shard_map/ppermute | solution.py:371
  110.6 1.6 %late_composites.2 = (f32[256,512]{1,0:T(8,128)S(1)}, f32[16,512]{1,0:T(8,128)S(1)}) custom-call(s32[3]{0:T(128)S(1)} %pad_add_fusion.core.place, bf16[8,64,512]{2,1,0:T(8,128)(2,1)S(1)} %collective-permute-done.9.far, bf16[256,4096]{1,0:T(8,128)(2,1)S(1)} %get-tuple-element.42.refs_8_.zed, f32[256,128]{1,0:T(8,128)S(1)} %get-tuple-element.44.zsum, ...), custom_call_target="tpu_custom_call" | custom-call | flops 134217728 | bytes 4194304 | tf_op jit(solution)/shard_map/late_composites/pallas_call | solution.py:257
  112.2 8.2 %collective-permute-start.11 = (f32[256,512]{1,0:T(8,128)S(1)}, f32[256,512]{1,0:T(8,128)S(1)}, u32[]{:S(2)}, u32[]{:S(2)}) collective-permute-start(f32[256,512]{1,0:T(8,128)S(1)} %get-tuple-element.49), channel_id=1, source_target_pairs={{0,1},{1,0},{2,3},{3,2},{4,5},{5,4},{6,7},{7,6},{8,9},{9,8},{10,11... | collective-permute-start | bytes 1572872 | tf_op jit(solution)/shard_map/ppermute | solution.py:376
  120.4 1.4 %late_composites.3.mine = f32[256,512]{1,0:T(8,128)S(1)} custom-call(s32[3]{0:T(128)S(1)} %pad_add_fusion.core.place, bf16[8,64,512]{2,1,0:T(8,128)(2,1)S(1)} %collective-permute-done.9.far, bf16[256,4096]{1,0:T(8,128)(2,1)S(1)} %get-tuple-element.35.zed.refs_7_, f32[256,128]{1,0:T(8,128)S(1)} %get-tuple-element.40.zsum, ...), custom_call_target="tpu_custom_call" | custom-call | flops 134217728 | bytes 4194304 | tf_op jit(solution)/shard_map/late_composites/pallas_call | solution.py:257
  121.7 0.1 collective-permute-done.11.got
  121.9 1.8 %merge_halves.1 = f32[256,1024]{1,0:T(8,128)} custom-call(s32[3]{0:T(128)S(1)} %pad_add_fusion.core.place, f32[256,512]{1,0:T(8,128)S(1)} %late_composites.3.mine, f32[256,512]{1,0:T(8,128)S(1)} %collective-permute-done.11.got), custom_call_target="tpu_custom_call" | custom-call | flops 1048576 | bytes 2097152 | tf_op jit(solution)/shard_map/merge_halves/pallas_call | solution.py:292
Async XLA Ops:
  1.4 0.7 copy-start
  6.3 11.3 %copy-start.1 = (bf16[256,2048]{1,0:T(8,128)(2,1)}, bf16[256,2048]{1,0:T(8,128)(2,1)S(1)}, u32[]{:S(2)}) copy-start(bf16[256,2048]{1,0:T(8,128)(2,1)S(1)} %get-tuple-element.31) | copy-start | bytes 3145732
  6.3 10.3 %collective-permute-start = (bf16[8,64,512]{2,1,0:T(8,128)(2,1)S(1)}, bf16[8,64,512]{2,1,0:T(8,128)(2,1)S(1)}, u32[]{:S(2)}, u32[]{:S(2)}) collective-permute-start(bf16[8,64,512]{2,1,0:T(8,128)(2,1)S(1)} %get-tuple-element.27), channel_id=1, source_target_pairs={{0,1},{1,0},{2,3},{3,2},{4,5},{5,4},{6,7},{7,6},{8,9},{9,8},{10,11... | collective-permute-start | bytes 1572872 | tf_op jit(solution)/shard_map/ppermute | solution.py:348
  17.6 20.9 %all-to-all-start = ((bf16[32,16,512]{2,1,0:T(8,128)(2,1)}), bf16[32,16,512]{2,1,0:T(8,128)(2,1)S(1)}, u32[]{:S(2)}, u32[]{:S(2)}) async-start(bf16[32,16,512]{2,1,0:T(8,128)(2,1)} %bitcast.4), calls=%async_computation | async-start | bytes 1048576 | tf_op jit(solution)/shard_map/all_to_all | solution.py:354
  21.9 22.5 %collective-permute-start.1 = (bf16[256,2048]{1,0:T(8,128)(2,1)}, bf16[256,2048]{1,0:T(8,128)(2,1)}, u32[]{:S(2)}, u32[]{:S(2)}) collective-permute-start(bf16[256,2048]{1,0:T(8,128)(2,1)} %copy-done.1), channel_id=1, source_target_pairs={{1,2},{3,4},{5,6},{7,8},{9,10},{11,12},{13,14},{15,16},{17,18},{19... | collective-permute-start | bytes 3145736 | tf_op jit(solution)/shard_map/ppermute | solution.py:353
  39.4 25.9 %all-to-all-start.1 = ((bf16[32,16,512]{2,1,0:T(8,128)(2,1)}), bf16[32,16,512]{2,1,0:T(8,128)(2,1)S(1)}, u32[]{:S(2)}, u32[]{:S(2)}) async-start(bf16[32,16,512]{2,1,0:T(8,128)(2,1)} %sum_and_spread.1), calls=%async_computation.1 | async-start | bytes 1048576 | tf_op jit(solution)/shard_map/all_to_all | solution.py:361
  46.7 43.3 %collective-permute-start.5 = (bf16[256,4096]{1,0:T(8,128)(2,1)S(1)}, bf16[256,4096]{1,0:T(8,128)(2,1)}, u32[]{:S(2)}, u32[]{:S(2)}) collective-permute-start(bf16[256,4096]{1,0:T(8,128)(2,1)S(1)} %get-tuple-element.35.zed.refs_7_), channel_id=1, source_target_pairs={{0,1},{1,0},{2,3},{3,2},{4,5},{5,4},{6,7},{7,6},{8,9},{9,8},{10,11... | collective-permute-start | bytes 6291464 | tf_op jit(solution)/shard_map/ppermute | solution.py:360
  58.5 6.7 %collective-permute-start.2 = (bf16[256,256]{1,0:T(8,128)(2,1)S(1)}, bf16[256,256]{1,0:T(8,128)(2,1)S(1)}, u32[]{:S(2)}, u32[]{:S(2)}) collective-permute-start(bf16[256,256]{1,0:T(8,128)(2,1)S(1)} %get-tuple-element.33), channel_id=1, source_target_pairs={{1,2},{3,4},{5,6},{7,8},{9,10},{11,12},{13,14},{15,16},{17,18},{19... | collective-permute-start | bytes 393224 | tf_op jit(solution)/shard_map/ppermute | solution.py:359
  65.2 11.4 %collective-permute-start.6 = (bf16[8,64,512]{2,1,0:T(8,128)(2,1)S(1)}, bf16[8,64,512]{2,1,0:T(8,128)(2,1)S(1)}, u32[]{:S(2)}, u32[]{:S(2)}) collective-permute-start(bf16[8,64,512]{2,1,0:T(8,128)(2,1)S(1)} %bitcast.6), channel_id=1, source_target_pairs={{0,8},{1,65},{2,10},{3,67},{4,12},{5,69},{6,14},{7,71},{8,16},{9,7... | collective-permute-start | bytes 1572872 | tf_op jit(solution)/shard_map/ppermute | solution.py:369
  68.9 10.2 %collective-permute-start.3 = (bf16[8,64,512]{2,1,0:T(8,128)(2,1)S(1)}, bf16[8,64,512]{2,1,0:T(8,128)(2,1)S(1)}, u32[]{:S(2)}, u32[]{:S(2)}) collective-permute-start(bf16[8,64,512]{2,1,0:T(8,128)(2,1)S(1)} %bitcast.7), channel_id=1, source_target_pairs={{8,0},{65,1},{10,2},{67,3},{12,4},{69,5},{14,6},{71,7},{16,8},{73,... | collective-permute-start | bytes 1572872 | tf_op jit(solution)/shard_map/ppermute | solution.py:370
  76.7 11.4 %collective-permute-start.7 = (bf16[8,64,512]{2,1,0:T(8,128)(2,1)S(1)}, bf16[8,64,512]{2,1,0:T(8,128)(2,1)S(1)}, u32[]{:S(2)}, u32[]{:S(2)}) collective-permute-start(bf16[8,64,512]{2,1,0:T(8,128)(2,1)S(1)} %collective-permute-done.6.refs_1_), channel_id=1, source_target_pairs={{0,8},{1,65},{2,10},{3,67},{4,12},{5,69},{6,14},{7,71},{8,16},{9,7... | collective-permute-start | bytes 1572872 | tf_op jit(solution)/shard_map/ppermute | solution.py:369
  79.1 14.2 %collective-permute-start.4 = (bf16[8,64,512]{2,1,0:T(8,128)(2,1)S(1)}, bf16[8,64,512]{2,1,0:T(8,128)(2,1)S(1)}, u32[]{:S(2)}, u32[]{:S(2)}) collective-permute-start(bf16[8,64,512]{2,1,0:T(8,128)(2,1)S(1)} %collective-permute-done.3.refs_2_), channel_id=1, source_target_pairs={{8,0},{65,1},{10,2},{67,3},{12,4},{69,5},{14,6},{71,7},{16,8},{73,... | collective-permute-start | bytes 1572872 | tf_op jit(solution)/shard_map/ppermute | solution.py:370
  88.1 11.4 %collective-permute-start.8 = (bf16[8,64,512]{2,1,0:T(8,128)(2,1)S(1)}, bf16[8,64,512]{2,1,0:T(8,128)(2,1)S(1)}, u32[]{:S(2)}, u32[]{:S(2)}) collective-permute-start(bf16[8,64,512]{2,1,0:T(8,128)(2,1)S(1)} %collective-permute-done.7.refs_3_), channel_id=1, source_target_pairs={{0,8},{1,65},{2,10},{3,67},{4,12},{5,69},{6,14},{7,71},{8,16},{9,7... | collective-permute-start | bytes 1572872 | tf_op jit(solution)/shard_map/ppermute | solution.py:369
  93.3 10.7 %collective-permute-start.10 = (bf16[8,64,512]{2,1,0:T(8,128)(2,1)S(1)}, bf16[8,64,512]{2,1,0:T(8,128)(2,1)S(1)}, u32[]{:S(2)}, u32[]{:S(2)}) collective-permute-start(bf16[8,64,512]{2,1,0:T(8,128)(2,1)S(1)} %collective-permute-done.4.refs_4_), channel_id=1, source_target_pairs={{8,0},{65,1},{10,2},{67,3},{12,4},{69,5},{14,6},{71,7},{16,8},{73,... | collective-permute-start | bytes 1572872 | tf_op jit(solution)/shard_map/ppermute | solution.py:370
  99.5 11.1 %collective-permute-start.9 = (bf16[8,64,512]{2,1,0:T(8,128)(2,1)S(1)}, bf16[8,64,512]{2,1,0:T(8,128)(2,1)S(1)}, u32[]{:S(2)}, u32[]{:S(2)}) collective-permute-start(bf16[8,64,512]{2,1,0:T(8,128)(2,1)S(1)} %collective-permute-done.8.refs_5_), channel_id=1, source_target_pairs={{0,8},{1,65},{2,10},{3,67},{4,12},{5,69},{6,14},{7,71},{8,16},{9,7... | collective-permute-start | bytes 1572872 | tf_op jit(solution)/shard_map/ppermute | solution.py:371
  112.2 9.7 %collective-permute-start.11 = (f32[256,512]{1,0:T(8,128)S(1)}, f32[256,512]{1,0:T(8,128)S(1)}, u32[]{:S(2)}, u32[]{:S(2)}) collective-permute-start(f32[256,512]{1,0:T(8,128)S(1)} %get-tuple-element.49), channel_id=1, source_target_pairs={{0,1},{1,0},{2,3},{3,2},{4,5},{5,4},{6,7},{7,6},{8,9},{9,8},{10,11... | collective-permute-start | bytes 1572872 | tf_op jit(solution)/shard_map/ppermute | solution.py:376

commit v4 on v3

--- a/solution.py
+++ b/solution.py
@@ -343,6 +343,9 @@
     every = ("z", "y", "x", "c")
     together = lax.optimization_barrier
     groups, up, down = groups_and_rings()
+    step_up = dict(up)
+    up_2 = [(i, step_up[j]) for i, j in up]
+    down_2 = [(j, i) for i, j in up_2]
     zed, edge, own, theirs = make_zed(station_count, place, composite_of.reshape(1, SLOTS), anomalies)
 
     got = lax.ppermute(theirs, "c", swap)
@@ -355,20 +358,16 @@
     spread = sum_and_spread(blocks)
 
     near_mine, near_theirs, zsum = make_edge(place, zed, halo)
-    near_theirs, zed = together((near_theirs, zed))
     near_got = lax.ppermute(near_theirs, every[1:], across)
+    first = lax.all_to_all(spread, every, split_axis=0, concat_axis=0, axis_index_groups=groups, tiled=True)
+    first, near_got, zed = together((first.reshape(8, HALF, CHUNK), near_got, zed))
     other = lax.ppermute(zed, "c", swap)
-    first = lax.all_to_all(spread, every, split_axis=0, concat_axis=0, axis_index_groups=groups, tiled=True)
-    first, near_got = together((first.reshape(8, HALF, CHUNK), near_got))
-
-    above, below = [first], [first]
-    for step in range(3):
-        if step == 2:
-            near_corr, osum, other = make_near(place, zed, other, near_mine, near_got)
-            below[2], near_corr = together((below[2], near_corr))
-        above.append(lax.ppermute(above[step], every, up))
-        below.append(lax.ppermute(below[step], every, down))
-    far = lax.ppermute(above[3], every, up)
+
+    near_1, near_2, far_1, far_2 = (lax.ppermute(first, every, ring) for ring in (up, down, up_2, down_2))
+    above = [first, near_1, far_1, lax.ppermute(far_1, every, up)]
+    far = lax.ppermute(far_1, every, up_2)
+    below = [first, near_2, far_2, lax.ppermute(far_2, every, down)]
+    near_corr, osum, other = make_near(place, zed, other, near_mine, near_got)
 
     blocks = [first, above[1], below[1], above[2], below[2], above[3], below[3]]
     early = make_early(place, blocks, zed, other)

time: 124 us -> 121 us (0.976)
  waiting for transfers between devices: 35.2 us -> 31.7 us
    ppermute x1, starting transfers between devices: 3.32 us -> 13.2 us  [per_device(): near_got = lax.ppermute(near_theirs, every[1:], across)]
    ppermute x1, starting transfers between devices: 11.8 us -> 6.03 us  [per_device(): other = lax.ppermute(zed, 'c', swap)]
    ppermute x7, waiting for transfers between devices: 17.6 us -> 13.4 us  [the longest x1 6.83 us: per_device(): far = lax.ppermute(far_1, every, up_2)]
    ppermute x1, starting transfers between devices: 8.15 us -> 4.23 us  [per_device(): back = lax.ppermute(for_other, 'c', swap)]
  transfers between devices with their start and end apart: 14 -> 14, of which waited for: 9 -> 7; matrix products, arithmetic and copies ran while one was open for 0% -> 0% of each run, Pallas kernels for 9% -> 8%
where the time goes in v4:
time: 121 us; the launch traced here: 120 us
  starting transfers between devices  67.7 us (56%)
  waiting for transfers between devices  31.7 us (26%)
  Pallas kernels  17.7 us (15%)
  between operations  1.47 us (1%)
    ppermute x1, starting transfers between devices, per_device(): near_got = lax.ppermute(near_theirs, every[1:], across)  13.2 us
    ppermute x4, starting transfers between devices, per_device(): lax.ppermute(first, every, ring)  12.7 us
    all_to_all x1, waiting for transfers between devices, per_device(): lax.all_to_all(part, ('y', 'x'), split_axis=0, concat_axis=0, tiled=True)  12.6 us
    ppermute x1, starting transfers between devices, per_device(): got = lax.ppermute(theirs, 'c', swap)  8.78 us
    ppermute x1, waiting for transfers between devices, per_device(): far = lax.ppermute(far_1, every, up_2)  6.83 us
    ppermute x1, starting transfers between devices, per_device(): other = lax.ppermute(zed, 'c', swap)  6.03 us
    all_to_all x1, starting transfers between devices, per_device(): lax.all_to_all(spread, every, split_axis=0, concat_axis=0, axis_index_gro...  4.98 us
    ppermute x1, starting transfers between devices, per_device(): above = [first, near_1, far_1, lax.ppermute(far_1, every, up)]  4.36 us
  transfers between devices with their start and end apart: 14, of which 7 were waited for; matrix products, arithmetic and copies ran while one was open for 0% of the time, Pallas kernels for 8%

profile of v4, /device:TPU:1, one launch (start us, length us, event | category | flops | bytes accessed | tf_op | source)
XLA Modules:
  0.0 120.3 jit_solution(6692162144930699559)
XLA Ops:
  1.3 0.1 pad_add_fusion.core.place
  1.4 0.0 copy-start
  1.4 0.7 copy-done
  2.0 4.3 %normalize_and_sum.1 = (bf16[256,4096]{1,0:T(8,128)(2,1)S(1)}, bf16[256,2048]{1,0:T(8,128)(2,1)S(1)}, f32[8,64,512]{2,1,0:T(8,128)S(1)}, bf16[8,64,512]{2,1,0:T(8,128)(2,1)S(1)}) custom-call(s32[1]{0:T(128)S(6)} %copy.5.count, s32[3]{0:T(128)S(1)} %pad_add_fusion.core.place, s32[1,256]{1,0:T(1,128)S(1)} %bitcast.11, bf16[256,4096]{1,0:T(8,128)(2,1)} %x.1), custom_call_target="tpu_custom_call" | custom-call | flops 300000000 | bytes 6291456 | tf_op jit(solution)/shard_map/normalize_and_sum/pallas_call | solution.py:73
  6.3 0.0 copy-start.1
  6.3 8.8 %collective-permute-start = (bf16[8,64,512]{2,1,0:T(8,128)(2,1)S(1)}, bf16[8,64,512]{2,1,0:T(8,128)(2,1)S(1)}, u32[]{:S(2)}, u32[]{:S(2)}) collective-permute-start(bf16[8,64,512]{2,1,0:T(8,128)(2,1)S(1)} %get-tuple-element.24), channel_id=1, source_target_pairs={{0,1},{1,0},{2,3},{3,2},{4,5},{5,4},{6,7},{7,6},{8,9},{9,8},{10,11... | collective-permute-start | bytes 1572872 | tf_op jit(solution)/shard_map/ppermute | solution.py:351
  15.1 1.5 %collective-permute-done = bf16[8,64,512]{2,1,0:T(8,128)(2,1)S(1)} collective-permute-done((bf16[8,64,512]{2,1,0:T(8,128)(2,1)S(1)}, bf16[8,64,512]{2,1,0:T(8,128)(2,1)S(1)}, u32[]{:S(2)}, u32[]{:S(2)}) %collective-permute-start) | collective-permute-done | bytes 524320 | tf_op jit(solution)/shard_map/ppermute | solution.py:351
  16.6 1.0 add_convert_fusion
  17.6 0.0 copy-done.1
  17.6 4.3 %all-to-all-start = ((bf16[32,16,512]{2,1,0:T(8,128)(2,1)}), bf16[32,16,512]{2,1,0:T(8,128)(2,1)S(1)}, u32[]{:S(2)}, u32[]{:S(2)}) async-start(bf16[32,16,512]{2,1,0:T(8,128)(2,1)} %bitcast.4), calls=%async_computation | async-start | bytes 1048576 | tf_op jit(solution)/shard_map/all_to_all | solution.py:357
  21.9 4.0 %collective-permute-start.1 = (bf16[256,2048]{1,0:T(8,128)(2,1)}, bf16[256,2048]{1,0:T(8,128)(2,1)}, u32[]{:S(2)}, u32[]{:S(2)}) collective-permute-start(bf16[256,2048]{1,0:T(8,128)(2,1)} %copy-done.1), channel_id=1, source_target_pairs={{1,2},{3,4},{5,6},{7,8},{9,10},{11,12},{13,14},{15,16},{17,18},{19... | collective-permute-start | bytes 3145736 | tf_op jit(solution)/shard_map/ppermute | solution.py:356
  25.9 12.6 %all-to-all-done.blocks = bf16[32,16,512]{2,1,0:T(8,128)(2,1)S(1)} async-done(((bf16[32,16,512]{2,1,0:T(8,128)(2,1)}), bf16[32,16,512]{2,1,0:T(8,128)(2,1)S(1)}, u32[]{:S(2)}, u32[]{:S(2)}) %all-to-all-start) | async-done | bytes 524320 | tf_op jit(solution)/shard_map/all_to_all | solution.py:357
  38.5 0.9 sum_and_spread.1
  39.4 5.0 %all-to-all-start.1 = ((bf16[32,16,512]{2,1,0:T(8,128)(2,1)}), bf16[32,16,512]{2,1,0:T(8,128)(2,1)S(1)}, u32[]{:S(2)}, u32[]{:S(2)}) async-start(bf16[32,16,512]{2,1,0:T(8,128)(2,1)} %sum_and_spread.1), calls=%async_computation.1 | async-start | bytes 1048576 | tf_op jit(solution)/shard_map/all_to_all | solution.py:362
  44.4 0.0 collective-permute-done.1.halo
  44.4 2.3 %edge_products.1 = (f32[256,256]{1,0:T(8,128)S(1)}, bf16[256,256]{1,0:T(8,128)(2,1)S(1)}, f32[256,128]{1,0:T(8,128)S(1)}) custom-call(s32[3]{0:T(128)S(1)} %pad_add_fusion.core.place, bf16[256,4096]{1,0:T(8,128)(2,1)S(1)} %get-tuple-element.30.zed.refs_7_, bf16[256,2048]{1,0:T(8,128)(2,1)} %collective-permute-done.1.halo), custom_call_target="tpu_custom_call" | custom-call | flops 536870912 | bytes 4194304 | tf_op jit(solution)/shard_map/edge_products/pallas_call | solution.py:115
  46.7 13.2 %collective-permute-start.2 = (bf16[256,256]{1,0:T(8,128)(2,1)S(1)}, bf16[256,256]{1,0:T(8,128)(2,1)S(1)}, u32[]{:S(2)}, u32[]{:S(2)}) collective-permute-start(bf16[256,256]{1,0:T(8,128)(2,1)S(1)} %get-tuple-element.29), channel_id=1, source_target_pairs={{1,2},{3,4},{5,6},{7,8},{9,10},{11,12},{13,14},{15,16},{17,18},{19... | collective-permute-start | bytes 393224 | tf_op jit(solution)/shard_map/ppermute | solution.py:361
  59.9 4.0 %collective-permute-done.2.got = bf16[256,256]{1,0:T(8,128)(2,1)S(1)} collective-permute-done((bf16[256,256]{1,0:T(8,128)(2,1)S(1)}, bf16[256,256]{1,0:T(8,128)(2,1)S(1)}, u32[]{:S(2)}, u32[]{:S(2)}) %collective-permute-start.2) | collective-permute-done | bytes 131104 | tf_op jit(solution)/shard_map/ppermute | solution.py:361
  64.0 0.0 all-to-all-done.1
  64.0 6.0 %collective-permute-start.3 = (bf16[256,4096]{1,0:T(8,128)(2,1)S(1)}, bf16[256,4096]{1,0:T(8,128)(2,1)S(1)}, u32[]{:S(2)}, u32[]{:S(2)}) collective-permute-start(bf16[256,4096]{1,0:T(8,128)(2,1)S(1)} %get-tuple-element.30.zed.refs_7_), channel_id=1, source_target_pairs={{0,1},{1,0},{2,3},{3,2},{4,5},{5,4},{6,7},{7,6},{8,9},{9,8},{10,11... | collective-permute-start | bytes 6291464 | tf_op jit(solution)/shard_map/ppermute | solution.py:364
  70.0 2.9 %collective-permute-start.8 = (bf16[8,64,512]{2,1,0:T(8,128)(2,1)S(1)}, bf16[8,64,512]{2,1,0:T(8,128)(2,1)S(1)}, u32[]{:S(2)}, u32[]{:S(2)}) collective-permute-start(bf16[8,64,512]{2,1,0:T(8,128)(2,1)S(1)} %bitcast.6), channel_id=1, source_target_pairs={{16,0},{129,1},{18,2},{131,3},{20,4},{133,5},{22,6},{135,7},{24,8}... | collective-permute-start | bytes 1572872 | tf_op jit(solution)/shard_map/ppermute | solution.py:366
  72.9 3.3 %collective-permute-start.4 = (bf16[8,64,512]{2,1,0:T(8,128)(2,1)S(1)}, bf16[8,64,512]{2,1,0:T(8,128)(2,1)S(1)}, u32[]{:S(2)}, u32[]{:S(2)}) collective-permute-start(bf16[8,64,512]{2,1,0:T(8,128)(2,1)S(1)} %bitcast.7), channel_id=1, source_target_pairs={{0,16},{1,129},{2,18},{3,131},{4,20},{5,133},{6,22},{7,135},{8,24}... | collective-permute-start | bytes 1572872 | tf_op jit(solution)/shard_map/ppermute | solution.py:366
  76.2 2.7 %collective-permute-start.6 = (bf16[8,64,512]{2,1,0:T(8,128)(2,1)S(1)}, bf16[8,64,512]{2,1,0:T(8,128)(2,1)S(1)}, u32[]{:S(2)}, u32[]{:S(2)}) collective-permute-start(bf16[8,64,512]{2,1,0:T(8,128)(2,1)S(1)} %bitcast.8), channel_id=1, source_target_pairs={{0,8},{1,65},{2,10},{3,67},{4,12},{5,69},{6,14},{7,71},{8,16},{9,7... | collective-permute-start | bytes 1572872 | tf_op jit(solution)/shard_map/ppermute | solution.py:366
  78.9 3.8 %collective-permute-start.7 = (bf16[8,64,512]{2,1,0:T(8,128)(2,1)S(1)}, bf16[8,64,512]{2,1,0:T(8,128)(2,1)S(1)}, u32[]{:S(2)}, u32[]{:S(2)}) collective-permute-start(bf16[8,64,512]{2,1,0:T(8,128)(2,1)S(1)} %bitcast.9), channel_id=1, source_target_pairs={{8,0},{65,1},{10,2},{67,3},{12,4},{69,5},{14,6},{71,7},{16,8},{73,... | collective-permute-start | bytes 1572872 | tf_op jit(solution)/shard_map/ppermute | solution.py:366
  82.7 4.1 %collective-permute-done.8.refs_4_ = bf16[8,64,512]{2,1,0:T(8,128)(2,1)S(1)} collective-permute-done((bf16[8,64,512]{2,1,0:T(8,128)(2,1)S(1)}, bf16[8,64,512]{2,1,0:T(8,128)(2,1)S(1)}, u32[]{:S(2)}, u32[]{:S(2)}) %collective-permute-start.8) | collective-permute-done | bytes 524320 | tf_op jit(solution)/shard_map/ppermute | solution.py:366
  86.8 1.9 %collective-permute-start.10 = (bf16[8,64,512]{2,1,0:T(8,128)(2,1)S(1)}, bf16[8,64,512]{2,1,0:T(8,128)(2,1)S(1)}, u32[]{:S(2)}, u32[]{:S(2)}) collective-permute-start(bf16[8,64,512]{2,1,0:T(8,128)(2,1)S(1)} %collective-permute-done.8.refs_4_), channel_id=1, source_target_pairs={{8,0},{65,1},{10,2},{67,3},{12,4},{69,5},{14,6},{71,7},{16,8},{73,... | collective-permute-start | bytes 1572872 | tf_op jit(solution)/shard_map/ppermute | solution.py:369
  88.7 0.0 collective-permute-done.4.refs_3_
  88.7 4.4 %collective-permute-start.9 = (bf16[8,64,512]{2,1,0:T(8,128)(2,1)S(1)}, bf16[8,64,512]{2,1,0:T(8,128)(2,1)S(1)}, u32[]{:S(2)}, u32[]{:S(2)}) collective-permute-start(bf16[8,64,512]{2,1,0:T(8,128)(2,1)S(1)} %collective-permute-done.4.refs_3_), channel_id=1, source_target_pairs={{0,8},{1,65},{2,10},{3,67},{4,12},{5,69},{6,14},{7,71},{8,16},{9,7... | collective-permute-start | bytes 1572872 | tf_op jit(solution)/shard_map/ppermute | solution.py:367
  93.1 0.0 collective-permute-done.3.other
  93.1 3.3 %collective-permute-start.5 = (bf16[8,64,512]{2,1,0:T(8,128)(2,1)S(1)}, bf16[8,64,512]{2,1,0:T(8,128)(2,1)S(1)}, u32[]{:S(2)}, u32[]{:S(2)}) collective-permute-start(bf16[8,64,512]{2,1,0:T(8,128)(2,1)S(1)} %collective-permute-done.4.refs_3_), channel_id=1, source_target_pairs={{0,16},{1,129},{2,18},{3,131},{4,20},{5,133},{6,22},{7,135},{8,24}... | collective-permute-start | bytes 1572872 | tf_op jit(solution)/shard_map/ppermute | solution.py:368
  96.4 2.4 %neighbour_correlation.1 = (f32[256,512]{1,0:T(8,128)}, f32[256,128]{1,0:T(8,128)S(1)}, bf16[256,4096]{1,0:T(8,128)(2,1)S(1)}) custom-call(s32[3]{0:T(128)S(1)} %pad_add_fusion.core.place, bf16[256,4096]{1,0:T(8,128)(2,1)S(1)} %get-tuple-element.30.zed.refs_7_, bf16[256,4096]{1,0:T(8,128)(2,1)S(1)} %collective-permute-done.3.other, ...), custom_call_target="tpu_custom_call" | custom-call | flops 536870912 | bytes 5242880 | tf_op jit(solution)/shard_map/neighbour_correlation/pallas_call | solution.py:135
  98.8 0.0 collective-permute-done.6.refs_1_
  98.8 0.0 collective-permute-done.7.refs_2_
  98.8 0.0 collective-permute-done.10.refs_6_
  98.8 2.5 %collective-permute-done.9.refs_5_ = bf16[8,64,512]{2,1,0:T(8,128)(2,1)S(1)} collective-permute-done((bf16[8,64,512]{2,1,0:T(8,128)(2,1)S(1)}, bf16[8,64,512]{2,1,0:T(8,128)(2,1)S(1)}, u32[]{:S(2)}, u32[]{:S(2)}) %collective-permute-start.9) | collective-permute-done | bytes 524320 | tf_op jit(solution)/shard_map/ppermute | solution.py:367
  101.2 3.1 %early_composites.1 = (f32[256,512]{1,0:T(8,128)S(1)}, f32[256,512]{1,0:T(8,128)S(1)}, f32[512,128]{1,0:T(8,128)S(1)}, f32[512,128]{1,0:T(8,128)S(1)}) custom-call(s32[3]{0:T(128)S(1)} %pad_add_fusion.core.place, bf16[8,64,512]{2,1,0:T(8,128)(2,1)S(1)} %bitcast.10, bf16[8,64,512]{2,1,0:T(8,128)(2,1)S(1)} %collective-permute-done.6.refs_1_, ...), custom_call_target="tpu_custom_call" | custom-call | flops 2013265920 | bytes 9437184 | tf_op jit(solution)/shard_map/early_composites/pallas_call | solution.py:242
  104.3 6.8 %collective-permute-done.5.far = bf16[8,64,512]{2,1,0:T(8,128)(2,1)S(1)} collective-permute-done((bf16[8,64,512]{2,1,0:T(8,128)(2,1)S(1)}, bf16[8,64,512]{2,1,0:T(8,128)(2,1)S(1)}, u32[]{:S(2)}, u32[]{:S(2)}) %collective-permute-start.5) | collective-permute-done | bytes 524320 | tf_op jit(solution)/shard_map/ppermute | solution.py:368
  111.2 1.6 %late_composites.2 = (f32[256,512]{1,0:T(8,128)S(1)}, f32[16,512]{1,0:T(8,128)S(1)}) custom-call(s32[3]{0:T(128)S(1)} %pad_add_fusion.core.place, bf16[8,64,512]{2,1,0:T(8,128)(2,1)S(1)} %collective-permute-done.5.far, bf16[256,4096]{1,0:T(8,128)(2,1)S(1)} %get-tuple-element.36.refs_8_.zed, f32[256,128]{1,0:T(8,128)S(1)} %get-tuple-element.38.zsum, ...), custom_call_target="tpu_custom_call" | custom-call | flops 134217728 | bytes 4194304 | tf_op jit(solution)/shard_map/late_composites/pallas_call | solution.py:257
  112.7 4.2 %collective-permute-start.11 = (f32[256,512]{1,0:T(8,128)S(1)}, f32[256,512]{1,0:T(8,128)S(1)}, u32[]{:S(2)}, u32[]{:S(2)}) collective-permute-start(f32[256,512]{1,0:T(8,128)S(1)} %get-tuple-element.43), channel_id=1, source_target_pairs={{0,1},{1,0},{2,3},{3,2},{4,5},{5,4},{6,7},{7,6},{8,9},{9,8},{10,11... | collective-permute-start | bytes 1572872 | tf_op jit(solution)/shard_map/ppermute | solution.py:375
  117.0 1.4 %late_composites.3.mine = f32[256,512]{1,0:T(8,128)S(1)} custom-call(s32[3]{0:T(128)S(1)} %pad_add_fusion.core.place, bf16[8,64,512]{2,1,0:T(8,128)(2,1)S(1)} %collective-permute-done.5.far, bf16[256,4096]{1,0:T(8,128)(2,1)S(1)} %get-tuple-element.30.zed.refs_7_, f32[256,128]{1,0:T(8,128)S(1)} %get-tuple-element.35.zsum, ...), custom_call_target="tpu_custom_call" | custom-call | flops 134217728 | bytes 4194304 | tf_op jit(solution)/shard_map/late_composites/pallas_call | solution.py:257
  118.4 0.1 collective-permute-done.11.got
  118.5 1.8 %merge_halves.1 = f32[256,1024]{1,0:T(8,128)} custom-call(s32[3]{0:T(128)S(1)} %pad_add_fusion.core.place, f32[256,512]{1,0:T(8,128)S(1)} %late_composites.3.mine, f32[256,512]{1,0:T(8,128)S(1)} %collective-permute-done.11.got), custom_call_target="tpu_custom_call" | custom-call | flops 1048576 | bytes 2097152 | tf_op jit(solution)/shard_map/merge_halves/pallas_call | solution.py:292
Async XLA Ops:
  1.4 0.7 copy-start
  6.3 11.3 %copy-start.1 = (bf16[256,2048]{1,0:T(8,128)(2,1)}, bf16[256,2048]{1,0:T(8,128)(2,1)S(1)}, u32[]{:S(2)}) copy-start(bf16[256,2048]{1,0:T(8,128)(2,1)S(1)} %get-tuple-element.28) | copy-start | bytes 3145732
  6.3 10.3 %collective-permute-start = (bf16[8,64,512]{2,1,0:T(8,128)(2,1)S(1)}, bf16[8,64,512]{2,1,0:T(8,128)(2,1)S(1)}, u32[]{:S(2)}, u32[]{:S(2)}) collective-permute-start(bf16[8,64,512]{2,1,0:T(8,128)(2,1)S(1)} %get-tuple-element.24), channel_id=1, source_target_pairs={{0,1},{1,0},{2,3},{3,2},{4,5},{5,4},{6,7},{7,6},{8,9},{9,8},{10,11... | collective-permute-start | bytes 1572872 | tf_op jit(solution)/shard_map/ppermute | solution.py:351
  17.6 20.9 %all-to-all-start = ((bf16[32,16,512]{2,1,0:T(8,128)(2,1)}), bf16[32,16,512]{2,1,0:T(8,128)(2,1)S(1)}, u32[]{:S(2)}, u32[]{:S(2)}) async-start(bf16[32,16,512]{2,1,0:T(8,128)(2,1)} %bitcast.4), calls=%async_computation | async-start | bytes 1048576 | tf_op jit(solution)/shard_map/all_to_all | solution.py:357
  21.9 22.5 %collective-permute-start.1 = (bf16[256,2048]{1,0:T(8,128)(2,1)}, bf16[256,2048]{1,0:T(8,128)(2,1)}, u32[]{:S(2)}, u32[]{:S(2)}) collective-permute-start(bf16[256,2048]{1,0:T(8,128)(2,1)} %copy-done.1), channel_id=1, source_target_pairs={{1,2},{3,4},{5,6},{7,8},{9,10},{11,12},{13,14},{15,16},{17,18},{19... | collective-permute-start | bytes 3145736 | tf_op jit(solution)/shard_map/ppermute | solution.py:356
  39.4 24.6 %all-to-all-start.1 = ((bf16[32,16,512]{2,1,0:T(8,128)(2,1)}), bf16[32,16,512]{2,1,0:T(8,128)(2,1)S(1)}, u32[]{:S(2)}, u32[]{:S(2)}) async-start(bf16[32,16,512]{2,1,0:T(8,128)(2,1)} %sum_and_spread.1), calls=%async_computation.1 | async-start | bytes 1048576 | tf_op jit(solution)/shard_map/all_to_all | solution.py:362
  46.7 17.3 %collective-permute-start.2 = (bf16[256,256]{1,0:T(8,128)(2,1)S(1)}, bf16[256,256]{1,0:T(8,128)(2,1)S(1)}, u32[]{:S(2)}, u32[]{:S(2)}) collective-permute-start(bf16[256,256]{1,0:T(8,128)(2,1)S(1)} %get-tuple-element.29), channel_id=1, source_target_pairs={{1,2},{3,4},{5,6},{7,8},{9,10},{11,12},{13,14},{15,16},{17,18},{19... | collective-permute-start | bytes 393224 | tf_op jit(solution)/shard_map/ppermute | solution.py:361
  64.0 29.1 %collective-permute-start.3 = (bf16[256,4096]{1,0:T(8,128)(2,1)S(1)}, bf16[256,4096]{1,0:T(8,128)(2,1)S(1)}, u32[]{:S(2)}, u32[]{:S(2)}) collective-permute-start(bf16[256,4096]{1,0:T(8,128)(2,1)S(1)} %get-tuple-element.30.zed.refs_7_), channel_id=1, source_target_pairs={{0,1},{1,0},{2,3},{3,2},{4,5},{5,4},{6,7},{7,6},{8,9},{9,8},{10,11... | collective-permute-start | bytes 6291464 | tf_op jit(solution)/shard_map/ppermute | solution.py:364
  70.0 16.8 %collective-permute-start.8 = (bf16[8,64,512]{2,1,0:T(8,128)(2,1)S(1)}, bf16[8,64,512]{2,1,0:T(8,128)(2,1)S(1)}, u32[]{:S(2)}, u32[]{:S(2)}) collective-permute-start(bf16[8,64,512]{2,1,0:T(8,128)(2,1)S(1)} %bitcast.6), channel_id=1, source_target_pairs={{16,0},{129,1},{18,2},{131,3},{20,4},{133,5},{22,6},{135,7},{24,8}... | collective-permute-start | bytes 1572872 | tf_op jit(solution)/shard_map/ppermute | solution.py:366
  72.9 15.8 %collective-permute-start.4 = (bf16[8,64,512]{2,1,0:T(8,128)(2,1)S(1)}, bf16[8,64,512]{2,1,0:T(8,128)(2,1)S(1)}, u32[]{:S(2)}, u32[]{:S(2)}) collective-permute-start(bf16[8,64,512]{2,1,0:T(8,128)(2,1)S(1)} %bitcast.7), channel_id=1, source_target_pairs={{0,16},{1,129},{2,18},{3,131},{4,20},{5,133},{6,22},{7,135},{8,24}... | collective-permute-start | bytes 1572872 | tf_op jit(solution)/shard_map/ppermute | solution.py:366
  76.2 22.5 %collective-permute-start.6 = (bf16[8,64,512]{2,1,0:T(8,128)(2,1)S(1)}, bf16[8,64,512]{2,1,0:T(8,128)(2,1)S(1)}, u32[]{:S(2)}, u32[]{:S(2)}) collective-permute-start(bf16[8,64,512]{2,1,0:T(8,128)(2,1)S(1)} %bitcast.8), channel_id=1, source_target_pairs={{0,8},{1,65},{2,10},{3,67},{4,12},{5,69},{6,14},{7,71},{8,16},{9,7... | collective-permute-start | bytes 1572872 | tf_op jit(solution)/shard_map/ppermute | solution.py:366
  78.9 19.9 %collective-permute-start.7 = (bf16[8,64,512]{2,1,0:T(8,128)(2,1)S(1)}, bf16[8,64,512]{2,1,0:T(8,128)(2,1)S(1)}, u32[]{:S(2)}, u32[]{:S(2)}) collective-permute-start(bf16[8,64,512]{2,1,0:T(8,128)(2,1)S(1)} %bitcast.9), channel_id=1, source_target_pairs={{8,0},{65,1},{10,2},{67,3},{12,4},{69,5},{14,6},{71,7},{16,8},{73,... | collective-permute-start | bytes 1572872 | tf_op jit(solution)/shard_map/ppermute | solution.py:366
  86.8 12.0 %collective-permute-start.10 = (bf16[8,64,512]{2,1,0:T(8,128)(2,1)S(1)}, bf16[8,64,512]{2,1,0:T(8,128)(2,1)S(1)}, u32[]{:S(2)}, u32[]{:S(2)}) collective-permute-start(bf16[8,64,512]{2,1,0:T(8,128)(2,1)S(1)} %collective-permute-done.8.refs_4_), channel_id=1, source_target_pairs={{8,0},{65,1},{10,2},{67,3},{12,4},{69,5},{14,6},{71,7},{16,8},{73,... | collective-permute-start | bytes 1572872 | tf_op jit(solution)/shard_map/ppermute | solution.py:369
  88.7 12.5 %collective-permute-start.9 = (bf16[8,64,512]{2,1,0:T(8,128)(2,1)S(1)}, bf16[8,64,512]{2,1,0:T(8,128)(2,1)S(1)}, u32[]{:S(2)}, u32[]{:S(2)}) collective-permute-start(bf16[8,64,512]{2,1,0:T(8,128)(2,1)S(1)} %collective-permute-done.4.refs_3_), channel_id=1, source_target_pairs={{0,8},{1,65},{2,10},{3,67},{4,12},{5,69},{6,14},{7,71},{8,16},{9,7... | collective-permute-start | bytes 1572872 | tf_op jit(solution)/shard_map/ppermute | solution.py:367
  93.1 18.0 %collective-permute-start.5 = (bf16[8,64,512]{2,1,0:T(8,128)(2,1)S(1)}, bf16[8,64,512]{2,1,0:T(8,128)(2,1)S(1)}, u32[]{:S(2)}, u32[]{:S(2)}) collective-permute-start(bf16[8,64,512]{2,1,0:T(8,128)(2,1)S(1)} %collective-permute-done.4.refs_3_), channel_id=1, source_target_pairs={{0,16},{1,129},{2,18},{3,131},{4,20},{5,133},{6,22},{7,135},{8,24}... | collective-permute-start | bytes 1572872 | tf_op jit(solution)/shard_map/ppermute | solution.py:368
  112.7 5.8 %collective-permute-start.11 = (f32[256,512]{1,0:T(8,128)S(1)}, f32[256,512]{1,0:T(8,128)S(1)}, u32[]{:S(2)}, u32[]{:S(2)}) collective-permute-start(f32[256,512]{1,0:T(8,128)S(1)} %get-tuple-element.43), channel_id=1, source_target_pairs={{0,1},{1,0},{2,3},{3,2},{4,5},{5,4},{6,7},{7,6},{8,9},{9,8},{10,11... | collective-permute-start | bytes 1572872 | tf_op jit(solution)/shard_map/ppermute | solution.py:375

commit v5 on v4

--- a/solution.py
+++ b/solution.py
@@ -188,7 +188,7 @@
             add(slice(k * CHUNK, (k + 1) * CHUNK), rows, k == 0)
 
 
-def late_kernel(here, place, far, zed, zsum, acc, *refs):
+def late_kernel(here, place, far_a, far_b, zed, zsum, acc, *refs):
     core, at = place[0], place[1]
     last = slice(COMPS - HALF, COMPS)
     if here:
@@ -199,7 +199,7 @@
 
     @pl.when(core == 0)
     def _():
-        rows = whole(far)
+        rows = jnp.concatenate([far_a[...], far_b[...]], axis=0).reshape(COMPS, CHUNK)
         out[...] = acc[...] + times(zed[:, hours_of(at, 4)], rows)
         if here:
             wide = rows.astype(F32)
@@ -211,7 +211,7 @@
         total = jnp.zeros((SLOTS, 128), F32)
         wide_1 = wide_2 = jnp.zeros((HALF, 128), F32)
         for k in range(NCHUNK):
-            rows = far[k]
+            rows = far_a[k] if k < 4 else far_b[k - 4]
             total = total + times(zed[:, k * CHUNK : (k + 1) * CHUNK], jnp.concatenate([rows, rows], axis=0))
             if here:
                 wide = rows.astype(F32)
@@ -256,14 +256,14 @@
     extra = list(sums) if here else [stats]
     return pl.pallas_call(
         functools.partial(late_kernel, here),
-        in_specs=[SMEM] + [VMEM] * (4 + len(extra)),
+        in_specs=[SMEM] + [VMEM] * (5 + len(extra)),
         out_specs=[VMEM] * (2 if here else 1),
         out_shape=[shape(SLOTS, COMPS)] + ([shape(16, COMPS)] if here else []),
         scratch_shapes=scratch,
         compiler_params=params(24),
         cost_estimate=pl.CostEstimate(flops=1 << 27, bytes_accessed=4 << 20, transcendentals=0),
         name="late_composites",
-    )(place, far, zed, zsum, acc, *extra)
+    )(place, *far, zed, zsum, acc, *extra)
 
 
 def merge_kernel(place, mine, got, out, held, sems):
@@ -365,7 +365,7 @@
 
     near_1, near_2, far_1, far_2 = (lax.ppermute(first, every, ring) for ring in (up, down, up_2, down_2))
     above = [first, near_1, far_1, lax.ppermute(far_1, every, up)]
-    far = lax.ppermute(far_1, every, up_2)
+    far = lax.ppermute(far_1[:4], every, up_2), lax.ppermute(far_2[4:], every, down_2)
     below = [first, near_2, far_2, lax.ppermute(far_2, every, down)]
     near_corr, osum, other = make_near(place, zed, other, near_mine, near_got)
 

time: 121 us -> 117 us (0.967)
  waiting for transfers between devices: 31.7 us -> 21.2 us
  starting transfers between devices: 67.7 us -> 74.1 us
    ppermute x1 -> x2, waiting for transfers between devices: 6.83 us -> 0.01 us  [the longest x1 0.01 us: per_device(): lax.ppermute(far_1[:4], every, up_2)]
    ppermute x1 -> x2, starting transfers between devices: 3.27 us -> 7.39 us  [the longest x1 5.47 us: per_device(): lax.ppermute(far_2[4:], every, down_2)]
    ppermute x1, waiting for transfers between devices: 2.48 us -> 0.01 us  [per_device(): above = [first, near_1, far_1, lax.ppermute(far_1, every, up)]]
    ppermute x1, starting transfers between devices: 1.91 us -> 4.11 us  [per_device(): below = [first, near_2, far_2, lax.ppermute(far_2, every, down)]]
    ppermute x4, starting transfers between devices: 12.7 us -> 13.9 us  [per_device(): lax.ppermute(first, every, ring)]
  transfers between devices with their start and end apart: 14 -> 15, of which waited for: 7 -> 5; matrix products, arithmetic and copies ran while one was open for 0% -> 0% of each run, Pallas kernels for 8% -> 9%
where the time goes in v5:
time: 117 us; the launch traced here: 116 us
  starting transfers between devices  74.1 us (63%)
  waiting for transfers between devices  21.2 us (18%)
  Pallas kernels  17.7 us (15%)
  between operations  1.52 us (1%)
    ppermute x4, starting transfers between devices, per_device(): lax.ppermute(first, every, ring)  13.9 us
    ppermute x1, starting transfers between devices, per_device(): near_got = lax.ppermute(near_theirs, every[1:], across)  13.2 us
    all_to_all x1, waiting for transfers between devices, per_device(): lax.all_to_all(part, ('y', 'x'), split_axis=0, concat_axis=0, tiled=True)  12.6 us
    ppermute x1, starting transfers between devices, per_device(): got = lax.ppermute(theirs, 'c', swap)  8.78 us
    ppermute x1, starting transfers between devices, per_device(): other = lax.ppermute(zed, 'c', swap)  6.03 us
    ppermute x1, starting transfers between devices, per_device(): lax.ppermute(far_2[4:], every, down_2)  5.47 us
    all_to_all x1, starting transfers between devices, per_device(): lax.all_to_all(spread, every, split_axis=0, concat_axis=0, axis_index_gro...  4.98 us
    all_to_all x1, starting transfers between devices, per_device(): lax.all_to_all(part, ('y', 'x'), split_axis=0, concat_axis=0, tiled=True)  4.3 us
  transfers between devices with their start and end apart: 15, of which 5 were waited for; matrix products, arithmetic and copies ran while one was open for 0% of the time, Pallas kernels for 9%

profile of v5, /device:TPU:1, one launch (start us, length us, event | category | flops | bytes accessed | tf_op | source)
XLA Modules:
  0.0 116.2 jit_solution(7647441238006838767)
XLA Ops:
  1.3 0.1 pad_add_fusion.core.place
  1.4 0.0 copy-start
  1.4 0.7 copy-done
  2.0 4.3 %normalize_and_sum.1 = (bf16[256,4096]{1,0:T(8,128)(2,1)S(1)}, bf16[256,2048]{1,0:T(8,128)(2,1)S(1)}, f32[8,64,512]{2,1,0:T(8,128)S(1)}, bf16[8,64,512]{2,1,0:T(8,128)(2,1)S(1)}) custom-call(s32[1]{0:T(128)S(6)} %copy.5.count, s32[3]{0:T(128)S(1)} %pad_add_fusion.core.place, s32[1,256]{1,0:T(1,128)S(1)} %bitcast.11, bf16[256,4096]{1,0:T(8,128)(2,1)} %x.1), custom_call_target="tpu_custom_call" | custom-call | flops 300000000 | bytes 6291456 | tf_op jit(solution)/shard_map/normalize_and_sum/pallas_call | solution.py:73
  6.3 0.0 copy-start.1
  6.3 8.8 %collective-permute-start = (bf16[8,64,512]{2,1,0:T(8,128)(2,1)S(1)}, bf16[8,64,512]{2,1,0:T(8,128)(2,1)S(1)}, u32[]{:S(2)}, u32[]{:S(2)}) collective-permute-start(bf16[8,64,512]{2,1,0:T(8,128)(2,1)S(1)} %get-tuple-element.24), channel_id=1, source_target_pairs={{0,1},{1,0},{2,3},{3,2},{4,5},{5,4},{6,7},{7,6},{8,9},{9,8},{10,11... | collective-permute-start | bytes 1572872 | tf_op jit(solution)/shard_map/ppermute | solution.py:351
  15.1 1.5 %collective-permute-done = bf16[8,64,512]{2,1,0:T(8,128)(2,1)S(1)} collective-permute-done((bf16[8,64,512]{2,1,0:T(8,128)(2,1)S(1)}, bf16[8,64,512]{2,1,0:T(8,128)(2,1)S(1)}, u32[]{:S(2)}, u32[]{:S(2)}) %collective-permute-start) | collective-permute-done | bytes 524320 | tf_op jit(solution)/shard_map/ppermute | solution.py:351
  16.6 1.0 add_convert_fusion
  17.6 0.0 copy-done.1
  17.6 4.3 %all-to-all-start = ((bf16[32,16,512]{2,1,0:T(8,128)(2,1)}), bf16[32,16,512]{2,1,0:T(8,128)(2,1)S(1)}, u32[]{:S(2)}, u32[]{:S(2)}) async-start(bf16[32,16,512]{2,1,0:T(8,128)(2,1)} %bitcast.4), calls=%async_computation | async-start | bytes 1048576 | tf_op jit(solution)/shard_map/all_to_all | solution.py:357
  21.9 4.0 %collective-permute-start.1 = (bf16[256,2048]{1,0:T(8,128)(2,1)}, bf16[256,2048]{1,0:T(8,128)(2,1)}, u32[]{:S(2)}, u32[]{:S(2)}) collective-permute-start(bf16[256,2048]{1,0:T(8,128)(2,1)} %copy-done.1), channel_id=1, source_target_pairs={{1,2},{3,4},{5,6},{7,8},{9,10},{11,12},{13,14},{15,16},{17,18},{19... | collective-permute-start | bytes 3145736 | tf_op jit(solution)/shard_map/ppermute | solution.py:356
  25.9 12.6 %all-to-all-done.blocks = bf16[32,16,512]{2,1,0:T(8,128)(2,1)S(1)} async-done(((bf16[32,16,512]{2,1,0:T(8,128)(2,1)}), bf16[32,16,512]{2,1,0:T(8,128)(2,1)S(1)}, u32[]{:S(2)}, u32[]{:S(2)}) %all-to-all-start) | async-done | bytes 524320 | tf_op jit(solution)/shard_map/all_to_all | solution.py:357
  38.5 0.9 sum_and_spread.1
  39.4 5.0 %all-to-all-start.1 = ((bf16[32,16,512]{2,1,0:T(8,128)(2,1)}), bf16[32,16,512]{2,1,0:T(8,128)(2,1)S(1)}, u32[]{:S(2)}, u32[]{:S(2)}) async-start(bf16[32,16,512]{2,1,0:T(8,128)(2,1)} %sum_and_spread.1), calls=%async_computation.1 | async-start | bytes 1048576 | tf_op jit(solution)/shard_map/all_to_all | solution.py:362
  44.4 0.0 collective-permute-done.1.halo
  44.4 2.3 %edge_products.1 = (f32[256,256]{1,0:T(8,128)S(1)}, bf16[256,256]{1,0:T(8,128)(2,1)S(1)}, f32[256,128]{1,0:T(8,128)S(1)}) custom-call(s32[3]{0:T(128)S(1)} %pad_add_fusion.core.place, bf16[256,4096]{1,0:T(8,128)(2,1)S(1)} %get-tuple-element.30.zed.refs_7_, bf16[256,2048]{1,0:T(8,128)(2,1)} %collective-permute-done.1.halo), custom_call_target="tpu_custom_call" | custom-call | flops 536870912 | bytes 4194304 | tf_op jit(solution)/shard_map/edge_products/pallas_call | solution.py:115
  46.7 13.2 %collective-permute-start.2 = (bf16[256,256]{1,0:T(8,128)(2,1)S(1)}, bf16[256,256]{1,0:T(8,128)(2,1)S(1)}, u32[]{:S(2)}, u32[]{:S(2)}) collective-permute-start(bf16[256,256]{1,0:T(8,128)(2,1)S(1)} %get-tuple-element.29), channel_id=1, source_target_pairs={{1,2},{3,4},{5,6},{7,8},{9,10},{11,12},{13,14},{15,16},{17,18},{19... | collective-permute-start | bytes 393224 | tf_op jit(solution)/shard_map/ppermute | solution.py:361
  59.9 4.0 %collective-permute-done.2.got = bf16[256,256]{1,0:T(8,128)(2,1)S(1)} collective-permute-done((bf16[256,256]{1,0:T(8,128)(2,1)S(1)}, bf16[256,256]{1,0:T(8,128)(2,1)S(1)}, u32[]{:S(2)}, u32[]{:S(2)}) %collective-permute-start.2) | collective-permute-done | bytes 131104 | tf_op jit(solution)/shard_map/ppermute | solution.py:361
  64.0 0.0 all-to-all-done.1
  64.0 6.0 %collective-permute-start.3 = (bf16[256,4096]{1,0:T(8,128)(2,1)S(1)}, bf16[256,4096]{1,0:T(8,128)(2,1)S(1)}, u32[]{:S(2)}, u32[]{:S(2)}) collective-permute-start(bf16[256,4096]{1,0:T(8,128)(2,1)S(1)} %get-tuple-element.30.zed.refs_7_), channel_id=1, source_target_pairs={{0,1},{1,0},{2,3},{3,2},{4,5},{5,4},{6,7},{7,6},{8,9},{9,8},{10,11... | collective-permute-start | bytes 6291464 | tf_op jit(solution)/shard_map/ppermute | solution.py:364
  70.0 3.1 %collective-permute-start.4 = (bf16[8,64,512]{2,1,0:T(8,128)(2,1)S(1)}, bf16[8,64,512]{2,1,0:T(8,128)(2,1)S(1)}, u32[]{:S(2)}, u32[]{:S(2)}) collective-permute-start(bf16[8,64,512]{2,1,0:T(8,128)(2,1)S(1)} %bitcast.6), channel_id=1, source_target_pairs={{0,16},{1,129},{2,18},{3,131},{4,20},{5,133},{6,22},{7,135},{8,24}... | collective-permute-start | bytes 1572872 | tf_op jit(solution)/shard_map/ppermute | solution.py:366
  73.1 4.3 %collective-permute-start.6 = (bf16[8,64,512]{2,1,0:T(8,128)(2,1)S(1)}, bf16[8,64,512]{2,1,0:T(8,128)(2,1)S(1)}, u32[]{:S(2)}, u32[]{:S(2)}) collective-permute-start(bf16[8,64,512]{2,1,0:T(8,128)(2,1)S(1)} %bitcast.7), channel_id=1, source_target_pairs={{16,0},{129,1},{18,2},{131,3},{20,4},{133,5},{22,6},{135,7},{24,8}... | collective-permute-start | bytes 1572872 | tf_op jit(solution)/shard_map/ppermute | solution.py:366
  77.4 2.7 %collective-permute-start.8 = (bf16[8,64,512]{2,1,0:T(8,128)(2,1)S(1)}, bf16[8,64,512]{2,1,0:T(8,128)(2,1)S(1)}, u32[]{:S(2)}, u32[]{:S(2)}) collective-permute-start(bf16[8,64,512]{2,1,0:T(8,128)(2,1)S(1)} %bitcast.8), channel_id=1, source_target_pairs={{0,8},{1,65},{2,10},{3,67},{4,12},{5,69},{6,14},{7,71},{8,16},{9,7... | collective-permute-start | bytes 1572872 | tf_op jit(solution)/shard_map/ppermute | solution.py:366
  80.1 3.8 %collective-permute-start.9 = (bf16[8,64,512]{2,1,0:T(8,128)(2,1)S(1)}, bf16[8,64,512]{2,1,0:T(8,128)(2,1)S(1)}, u32[]{:S(2)}, u32[]{:S(2)}) collective-permute-start(bf16[8,64,512]{2,1,0:T(8,128)(2,1)S(1)} %bitcast.9), channel_id=1, source_target_pairs={{8,0},{65,1},{10,2},{67,3},{12,4},{69,5},{14,6},{71,7},{16,8},{73,... | collective-permute-start | bytes 1572872 | tf_op jit(solution)/shard_map/ppermute | solution.py:366
  83.9 2.9 %collective-permute-done.4.refs_3_ = bf16[8,64,512]{2,1,0:T(8,128)(2,1)S(1)} collective-permute-done((bf16[8,64,512]{2,1,0:T(8,128)(2,1)S(1)}, bf16[8,64,512]{2,1,0:T(8,128)(2,1)S(1)}, u32[]{:S(2)}, u32[]{:S(2)}) %collective-permute-start.4) | collective-permute-done | bytes 524320 | tf_op jit(solution)/shard_map/ppermute | solution.py:366
  86.8 3.5 %collective-permute-start.10 = (bf16[8,64,512]{2,1,0:T(8,128)(2,1)S(1)}, bf16[8,64,512]{2,1,0:T(8,128)(2,1)S(1)}, u32[]{:S(2)}, u32[]{:S(2)}) collective-permute-start(bf16[8,64,512]{2,1,0:T(8,128)(2,1)S(1)} %collective-permute-done.4.refs_3_), channel_id=1, source_target_pairs={{0,8},{1,65},{2,10},{3,67},{4,12},{5,69},{6,14},{7,71},{8,16},{9,7... | collective-permute-start | bytes 1572872 | tf_op jit(solution)/shard_map/ppermute | solution.py:367
  90.4 0.0 collective-permute-done.6.refs_4_
  90.4 4.1 %collective-permute-start.11 = (bf16[8,64,512]{2,1,0:T(8,128)(2,1)S(1)}, bf16[8,64,512]{2,1,0:T(8,128)(2,1)S(1)}, u32[]{:S(2)}, u32[]{:S(2)}) collective-permute-start(bf16[8,64,512]{2,1,0:T(8,128)(2,1)S(1)} %collective-permute-done.6.refs_4_), channel_id=1, source_target_pairs={{8,0},{65,1},{10,2},{67,3},{12,4},{69,5},{14,6},{71,7},{16,8},{73,... | collective-permute-start | bytes 1572872 | tf_op jit(solution)/shard_map/ppermute | solution.py:369
  94.6 0.0 collective-permute-done.8.refs_1_
  94.6 1.9 %collective-permute-start.5 = (bf16[4,64,512]{2,1,0:T(8,128)(2,1)S(1)}, bf16[4,64,512]{2,1,0:T(8,128)(2,1)S(1)}, u32[]{:S(2)}, u32[]{:S(2)}) collective-permute-start(bf16[4,64,512]{2,1,0:T(8,128)(2,1)S(1)} %slice.8), channel_id=1, source_target_pairs={{0,16},{1,129},{2,18},{3,131},{4,20},{5,133},{6,22},{7,135},{8,24}... | collective-permute-start | bytes 786440 | tf_op jit(solution)/shard_map/ppermute | solution.py:368
  96.5 0.0 collective-permute-done.3.other
  96.5 5.5 %collective-permute-start.7 = (bf16[4,64,512]{2,1,0:T(8,128)(2,1)S(1)}, bf16[4,64,512]{2,1,0:T(8,128)(2,1)S(1)}, u32[]{:S(2)}, u32[]{:S(2)}) collective-permute-start(bf16[4,64,512]{2,1,0:T(8,128)(2,1)S(1)} %slice.9), channel_id=1, source_target_pairs={{16,0},{129,1},{18,2},{131,3},{20,4},{133,5},{22,6},{135,7},{24,8}... | collective-permute-start | bytes 786440 | tf_op jit(solution)/shard_map/ppermute | solution.py:368
  102.0 2.4 %neighbour_correlation.1 = (f32[256,512]{1,0:T(8,128)}, f32[256,128]{1,0:T(8,128)S(1)}, bf16[256,4096]{1,0:T(8,128)(2,1)S(1)}) custom-call(s32[3]{0:T(128)S(1)} %pad_add_fusion.core.place, bf16[256,4096]{1,0:T(8,128)(2,1)S(1)} %get-tuple-element.30.zed.refs_7_, bf16[256,4096]{1,0:T(8,128)(2,1)S(1)} %collective-permute-done.3.other, ...), custom_call_target="tpu_custom_call" | custom-call | flops 536870912 | bytes 5242880 | tf_op jit(solution)/shard_map/neighbour_correlation/pallas_call | solution.py:135
  104.4 0.0 collective-permute-done.9.refs_2_
  104.4 0.0 collective-permute-done.10.refs_5_
  104.4 0.0 collective-permute-done.11.refs_6_
  104.4 3.1 %early_composites.1 = (f32[256,512]{1,0:T(8,128)S(1)}, f32[256,512]{1,0:T(8,128)S(1)}, f32[512,128]{1,0:T(8,128)S(1)}, f32[512,128]{1,0:T(8,128)S(1)}) custom-call(s32[3]{0:T(128)S(1)} %pad_add_fusion.core.place, bf16[8,64,512]{2,1,0:T(8,128)(2,1)S(1)} %bitcast.10, bf16[8,64,512]{2,1,0:T(8,128)(2,1)S(1)} %collective-permute-done.8.refs_1_, ...), custom_call_target="tpu_custom_call" | custom-call | flops 2013265920 | bytes 9437184 | tf_op jit(solution)/shard_map/early_composites/pallas_call | solution.py:242
  107.5 0.0 collective-permute-done.5.far_a
  107.5 0.0 collective-permute-done.7.far_b
  107.5 1.6 %late_composites.2 = (f32[256,512]{1,0:T(8,128)S(1)}, f32[16,512]{1,0:T(8,128)S(1)}) custom-call(s32[3]{0:T(128)S(1)} %pad_add_fusion.core.place, bf16[4,64,512]{2,1,0:T(8,128)(2,1)S(1)} %collective-permute-done.5.far_a, bf16[4,64,512]{2,1,0:T(8,128)(2,1)S(1)} %collective-permute-done.7.far_b, bf16[256,4096]{1,0:T(8,128)(2,1)S(1)} %get-tuple-element.36.refs_8_.zed, ...), custom_call_target="tpu_custom_call" | custom-call | flops 134217728 | bytes 4194304 | tf_op jit(solution)/shard_map/late_composites/pallas_call | solution.py:257
  109.1 3.9 %collective-permute-start.12 = (f32[256,512]{1,0:T(8,128)S(1)}, f32[256,512]{1,0:T(8,128)S(1)}, u32[]{:S(2)}, u32[]{:S(2)}) collective-permute-start(f32[256,512]{1,0:T(8,128)S(1)} %get-tuple-element.43), channel_id=1, source_target_pairs={{0,1},{1,0},{2,3},{3,2},{4,5},{5,4},{6,7},{7,6},{8,9},{9,8},{10,11... | collective-permute-start | bytes 1572872 | tf_op jit(solution)/shard_map/ppermute | solution.py:375
  112.9 1.4 %late_composites.3.mine = f32[256,512]{1,0:T(8,128)S(1)} custom-call(s32[3]{0:T(128)S(1)} %pad_add_fusion.core.place, bf16[4,64,512]{2,1,0:T(8,128)(2,1)S(1)} %collective-permute-done.5.far_a, bf16[4,64,512]{2,1,0:T(8,128)(2,1)S(1)} %collective-permute-done.7.far_b, bf16[256,4096]{1,0:T(8,128)(2,1)S(1)} %get-tuple-element.30.zed.refs_7_, ...), custom_call_target="tpu_custom_call" | custom-call | flops 134217728 | bytes 4194304 | tf_op jit(solution)/shard_map/late_composites/pallas_call | solution.py:257
  114.3 0.1 collective-permute-done.12.got
  114.4 1.8 %merge_halves.1 = f32[256,1024]{1,0:T(8,128)} custom-call(s32[3]{0:T(128)S(1)} %pad_add_fusion.core.place, f32[256,512]{1,0:T(8,128)S(1)} %late_composites.3.mine, f32[256,512]{1,0:T(8,128)S(1)} %collective-permute-done.12.got), custom_call_target="tpu_custom_call" | custom-call | flops 1048576 | bytes 2097152 | tf_op jit(solution)/shard_map/merge_halves/pallas_call | solution.py:292
  (2 shorter events, 0.0 us)
Async XLA Ops:
  1.4 0.7 copy-start
  6.3 11.3 %copy-start.1 = (bf16[256,2048]{1,0:T(8,128)(2,1)}, bf16[256,2048]{1,0:T(8,128)(2,1)S(1)}, u32[]{:S(2)}) copy-start(bf16[256,2048]{1,0:T(8,128)(2,1)S(1)} %get-tuple-element.28) | copy-start | bytes 3145732
  6.3 10.3 %collective-permute-start = (bf16[8,64,512]{2,1,0:T(8,128)(2,1)S(1)}, bf16[8,64,512]{2,1,0:T(8,128)(2,1)S(1)}, u32[]{:S(2)}, u32[]{:S(2)}) collective-permute-start(bf16[8,64,512]{2,1,0:T(8,128)(2,1)S(1)} %get-tuple-element.24), channel_id=1, source_target_pairs={{0,1},{1,0},{2,3},{3,2},{4,5},{5,4},{6,7},{7,6},{8,9},{9,8},{10,11... | collective-permute-start | bytes 1572872 | tf_op jit(solution)/shard_map/ppermute | solution.py:351
  17.6 20.9 %all-to-all-start = ((bf16[32,16,512]{2,1,0:T(8,128)(2,1)}), bf16[32,16,512]{2,1,0:T(8,128)(2,1)S(1)}, u32[]{:S(2)}, u32[]{:S(2)}) async-start(bf16[32,16,512]{2,1,0:T(8,128)(2,1)} %bitcast.4), calls=%async_computation | async-start | bytes 1048576 | tf_op jit(solution)/shard_map/all_to_all | solution.py:357
  21.9 22.5 %collective-permute-start.1 = (bf16[256,2048]{1,0:T(8,128)(2,1)}, bf16[256,2048]{1,0:T(8,128)(2,1)}, u32[]{:S(2)}, u32[]{:S(2)}) collective-permute-start(bf16[256,2048]{1,0:T(8,128)(2,1)} %copy-done.1), channel_id=1, source_target_pairs={{1,2},{3,4},{5,6},{7,8},{9,10},{11,12},{13,14},{15,16},{17,18},{19... | collective-permute-start | bytes 3145736 | tf_op jit(solution)/shard_map/ppermute | solution.py:356
  39.4 24.6 %all-to-all-start.1 = ((bf16[32,16,512]{2,1,0:T(8,128)(2,1)}), bf16[32,16,512]{2,1,0:T(8,128)(2,1)S(1)}, u32[]{:S(2)}, u32[]{:S(2)}) async-start(bf16[32,16,512]{2,1,0:T(8,128)(2,1)} %sum_and_spread.1), calls=%async_computation.1 | async-start | bytes 1048576 | tf_op jit(solution)/shard_map/all_to_all | solution.py:362
  46.7 17.3 %collective-permute-start.2 = (bf16[256,256]{1,0:T(8,128)(2,1)S(1)}, bf16[256,256]{1,0:T(8,128)(2,1)S(1)}, u32[]{:S(2)}, u32[]{:S(2)}) collective-permute-start(bf16[256,256]{1,0:T(8,128)(2,1)S(1)} %get-tuple-element.29), channel_id=1, source_target_pairs={{1,2},{3,4},{5,6},{7,8},{9,10},{11,12},{13,14},{15,16},{17,18},{19... | collective-permute-start | bytes 393224 | tf_op jit(solution)/shard_map/ppermute | solution.py:361
  64.0 32.5 %collective-permute-start.3 = (bf16[256,4096]{1,0:T(8,128)(2,1)S(1)}, bf16[256,4096]{1,0:T(8,128)(2,1)S(1)}, u32[]{:S(2)}, u32[]{:S(2)}) collective-permute-start(bf16[256,4096]{1,0:T(8,128)(2,1)S(1)} %get-tuple-element.30.zed.refs_7_), channel_id=1, source_target_pairs={{0,1},{1,0},{2,3},{3,2},{4,5},{5,4},{6,7},{7,6},{8,9},{9,8},{10,11... | collective-permute-start | bytes 6291464 | tf_op jit(solution)/shard_map/ppermute | solution.py:364
  70.0 16.8 %collective-permute-start.4 = (bf16[8,64,512]{2,1,0:T(8,128)(2,1)S(1)}, bf16[8,64,512]{2,1,0:T(8,128)(2,1)S(1)}, u32[]{:S(2)}, u32[]{:S(2)}) collective-permute-start(bf16[8,64,512]{2,1,0:T(8,128)(2,1)S(1)} %bitcast.6), channel_id=1, source_target_pairs={{0,16},{1,129},{2,18},{3,131},{4,20},{5,133},{6,22},{7,135},{8,24}... | collective-permute-start | bytes 1572872 | tf_op jit(solution)/shard_map/ppermute | solution.py:366
  73.1 17.3 %collective-permute-start.6 = (bf16[8,64,512]{2,1,0:T(8,128)(2,1)S(1)}, bf16[8,64,512]{2,1,0:T(8,128)(2,1)S(1)}, u32[]{:S(2)}, u32[]{:S(2)}) collective-permute-start(bf16[8,64,512]{2,1,0:T(8,128)(2,1)S(1)} %bitcast.7), channel_id=1, source_target_pairs={{16,0},{129,1},{18,2},{131,3},{20,4},{133,5},{22,6},{135,7},{24,8}... | collective-permute-start | bytes 1572872 | tf_op jit(solution)/shard_map/ppermute | solution.py:366
  77.4 17.1 %collective-permute-start.8 = (bf16[8,64,512]{2,1,0:T(8,128)(2,1)S(1)}, bf16[8,64,512]{2,1,0:T(8,128)(2,1)S(1)}, u32[]{:S(2)}, u32[]{:S(2)}) collective-permute-start(bf16[8,64,512]{2,1,0:T(8,128)(2,1)S(1)} %bitcast.8), channel_id=1, source_target_pairs={{0,8},{1,65},{2,10},{3,67},{4,12},{5,69},{6,14},{7,71},{8,16},{9,7... | collective-permute-start | bytes 1572872 | tf_op jit(solution)/shard_map/ppermute | solution.py:366
  80.1 24.3 %collective-permute-start.9 = (bf16[8,64,512]{2,1,0:T(8,128)(2,1)S(1)}, bf16[8,64,512]{2,1,0:T(8,128)(2,1)S(1)}, u32[]{:S(2)}, u32[]{:S(2)}) collective-permute-start(bf16[8,64,512]{2,1,0:T(8,128)(2,1)S(1)} %bitcast.9), channel_id=1, source_target_pairs={{8,0},{65,1},{10,2},{67,3},{12,4},{69,5},{14,6},{71,7},{16,8},{73,... | collective-permute-start | bytes 1572872 | tf_op jit(solution)/shard_map/ppermute | solution.py:366
  86.8 17.5 %collective-permute-start.10 = (bf16[8,64,512]{2,1,0:T(8,128)(2,1)S(1)}, bf16[8,64,512]{2,1,0:T(8,128)(2,1)S(1)}, u32[]{:S(2)}, u32[]{:S(2)}) collective-permute-start(bf16[8,64,512]{2,1,0:T(8,128)(2,1)S(1)} %collective-permute-done.4.refs_3_), channel_id=1, source_target_pairs={{0,8},{1,65},{2,10},{3,67},{4,12},{5,69},{6,14},{7,71},{8,16},{9,7... | collective-permute-start | bytes 1572872 | tf_op jit(solution)/shard_map/ppermute | solution.py:367
  90.4 14.0 %collective-permute-start.11 = (bf16[8,64,512]{2,1,0:T(8,128)(2,1)S(1)}, bf16[8,64,512]{2,1,0:T(8,128)(2,1)S(1)}, u32[]{:S(2)}, u32[]{:S(2)}) collective-permute-start(bf16[8,64,512]{2,1,0:T(8,128)(2,1)S(1)} %collective-permute-done.6.refs_4_), channel_id=1, source_target_pairs={{8,0},{65,1},{10,2},{67,3},{12,4},{69,5},{14,6},{71,7},{16,8},{73,... | collective-permute-start | bytes 1572872 | tf_op jit(solution)/shard_map/ppermute | solution.py:369
  94.6 12.9 %collective-permute-start.5 = (bf16[4,64,512]{2,1,0:T(8,128)(2,1)S(1)}, bf16[4,64,512]{2,1,0:T(8,128)(2,1)S(1)}, u32[]{:S(2)}, u32[]{:S(2)}) collective-permute-start(bf16[4,64,512]{2,1,0:T(8,128)(2,1)S(1)} %slice.8), channel_id=1, source_target_pairs={{0,16},{1,129},{2,18},{3,131},{4,20},{5,133},{6,22},{7,135},{8,24}... | collective-permute-start | bytes 786440 | tf_op jit(solution)/shard_map/ppermute | solution.py:368
  96.5 11.0 %collective-permute-start.7 = (bf16[4,64,512]{2,1,0:T(8,128)(2,1)S(1)}, bf16[4,64,512]{2,1,0:T(8,128)(2,1)S(1)}, u32[]{:S(2)}, u32[]{:S(2)}) collective-permute-start(bf16[4,64,512]{2,1,0:T(8,128)(2,1)S(1)} %slice.9), channel_id=1, source_target_pairs={{16,0},{129,1},{18,2},{131,3},{20,4},{133,5},{22,6},{135,7},{24,8}... | collective-permute-start | bytes 786440 | tf_op jit(solution)/shard_map/ppermute | solution.py:368
  109.1 5.4 %collective-permute-start.12 = (f32[256,512]{1,0:T(8,128)S(1)}, f32[256,512]{1,0:T(8,128)S(1)}, u32[]{:S(2)}, u32[]{:S(2)}) collective-permute-start(f32[256,512]{1,0:T(8,128)S(1)} %get-tuple-element.43), channel_id=1, source_target_pairs={{0,1},{1,0},{2,3},{3,2},{4,5},{5,4},{6,7},{7,6},{8,9},{9,8},{10,11... | collective-permute-start | bytes 1572872 | tf_op jit(solution)/shard_map/ppermute | solution.py:375
